TPU v7x, 32 devices: a whole 2x2x4 slice. The times are simulated.
32 devices in a mesh: dp: 8 (over z, y), tensor: 4 (over x, core).
Axes of the slice: x: 2, y: 2, z: 4, core: 2. Of those that a mesh axis runs over, the one named last changes fastest.
Arguments:
- inputs: bfloat16 [8192, 768], P(('dp', 'tensor')), may hold values from -6 to 6
- segments: int32 [8, 1024], P('dp'), may hold values from 0 to 7, never falling along the last dimension, each value on 1 to 256 neighbouring positions
- buckets: int32 [2047], replicated, may hold values from 0 to 31
- routes: int32 [8, 1024, 1], P('dp'), may hold values from 0 to 15; in each aligned block of 1024 rows (0 to 1023, 1024 to 2047, ..., all dimensions but the last counted through in order) at most 80 rows name the same one
- qkv_weight: bfloat16 [3, 768, 768], P(None, None, 'tensor'), may hold values from -0.109375 to 0.109375
- out_weight: bfloat16 [768, 768], P('tensor'), may hold values from -0.75 to 0.75
- rel_bias: float32 [32, 12], P(None, 'tensor'), may hold values from -3 to 3
- norm_attn: float32 [768], replicated, may hold values from 0.5 to 1.5
- norm_moe: float32 [768], replicated, may hold values from 0.5 to 1.5
- router_weight: bfloat16 [768, 16], replicated, may hold values from -0.109375 to 0.109375
- expert_in: bfloat16 [16, 768, 3072], P('dp', None, 'tensor'), may hold values from -0.21875 to 0.21875
- expert_out: bfloat16 [16, 3072, 768], P('dp', 'tensor'), may hold values from -3.59375 to 3.59375
- cotangent: bfloat16 [8192, 768], P(('dp', 'tensor')), may hold values from -6 to 6
Outputs:
- output: bfloat16 [8192, 768], P(('dp', 'tensor'))
- grad_inputs: float32 [8192, 768], P(('dp', 'tensor'))
- grad_qkv_weight: float32 [3, 768, 768], P(None, None, 'tensor')
- grad_out_weight: float32 [768, 768], P('tensor')
- grad_rel_bias: float32 [32, 12], P(None, 'tensor')
- grad_norm_attn: float32 [768], replicated
- grad_norm_moe: float32 [768], replicated
- grad_router: float32 [768, 16], replicated
- grad_expert_in: float32 [16, 768, 3072], P('dp', None, 'tensor')
- grad_expert_out: float32 [16, 3072, 768], P('dp', 'tensor')
Inputs may be any that keep to these rules, and one draw needn't show every extreme that they name: `routes`: at most 80 tokens of one sequence have the same route, and in every draw some expert gets exactly 80 tokens of some sequence. `segments`: along a sequence the ids never fall; each document holds 1 to 256 positions.
All inputs are finite; a program needn't handle non-finite values.
Results may differ from a plain program's by a relative error of at most 0.018.
The roundings to bfloat16 on the way count: a program that leaves them out, or rounds other values in their place, can miss the bound.
Values may be sent and summed in bfloat16 or wider, within the bound.
No kernel may reach another device: no remote copies, remote signals or barrier semaphores. Data moves between devices by JAX's collectives and lax.ppermute only.
A program may use at most 192 MiB of HBM per device.

v0:
```python
import jax
import jax.numpy as jnp
from jax import lax
from jax.sharding import PartitionSpec as P

epsilon = 1e-06
negative = -1000000000.0


def smooth_act(values):
    return jax.nn.gelu(values, approximate=True)


def rms_apply(values, gain_vec):
    inv_rms = lax.rsqrt(jnp.mean(values * values, axis=-1, keepdims=True) + epsilon)
    return values * inv_rms * gain_vec


def skew_bias(dist_bias, row_start, block_rows, seq_rows):
    head_count = dist_bias.shape[0]
    length = seq_rows + block_rows - 1
    first = seq_rows - row_start - block_rows
    window = lax.slice_in_dim(dist_bias, first, first + length, axis=1)
    tiled = jnp.tile(window, (1, block_rows))
    cut = tiled[:, block_rows - 1 : block_rows - 1 + block_rows * (length - 1)]
    return cut.reshape(head_count, block_rows, length - 1)[:, :, :seq_rows]


def skew_back(grad_block, row_start, block_rows, seq_rows):
    head_count = grad_block.shape[0]
    length = seq_rows + block_rows - 1
    first = seq_rows - row_start - block_rows
    padded = jnp.pad(grad_block, ((0, 0), (0, 0), (0, length - 1 - seq_rows)))
    flat = padded.reshape(head_count, block_rows * (length - 1))
    flat = jnp.pad(flat, ((0, 0), (block_rows - 1, 1)))
    window = jnp.sum(flat.reshape(head_count, block_rows, length), axis=1)
    return jnp.pad(window, ((0, 0), (first, 2 * seq_rows - 1 - first - length)))


def rows_of(dispatch, table):
    return lax.dot_general(
        dispatch, table, (((0,), (0,)), ((), ())), preferred_element_type=jnp.float32
    )


def to_tokens(expert_buffer, dispatch):
    returned = lax.all_to_all(expert_buffer, "dp", split_axis=1, concat_axis=0, tiled=True)
    returned = returned.reshape(-1, returned.shape[2])
    return lax.psum_scatter(
        rows_of(dispatch, returned).astype(jnp.bfloat16), "tensor", scatter_dimension=0, tiled=True
    ).astype(jnp.float32)


def per_device(
    inputs,
    segments,
    buckets,
    routes,
    qkv_weight,
    out_weight,
    rel_bias,
    norm_attn,
    norm_moe,
    router_weight,
    expert_in,
    expert_out,
    cotangent,
):
    own_rows = inputs.shape[0]
    width_model = inputs.shape[1]
    seq_rows = own_rows * lax.axis_size("tensor")
    expert_count = router_weight.shape[1]
    capacity = max(2, 5 * seq_rows // (4 * expert_count))
    slot_total = expert_count * capacity
    columns = qkv_weight.shape[2]
    head_count = rel_bias.shape[1]
    head_size = columns // head_count
    bucket_count = rel_bias.shape[0]
    block_rows = min(512, seq_rows)
    row_starts = list(range(0, seq_rows, block_rows))
    seg_row = segments[0]
    route_seq = routes[0, :, 0]
    own_start = lax.axis_index("tensor") * own_rows
    route_mine = lax.dynamic_slice_in_dim(route_seq, own_start, own_rows, 0)
    inputs_f32 = inputs.astype(jnp.float32)
    normed_attn = rms_apply(inputs_f32, norm_attn).astype(jnp.bfloat16)
    seq_normed = lax.all_gather(normed_attn, "tensor", axis=0, tiled=True)
    qkv = jnp.einsum(
        "sd,cdf->csf", seq_normed, qkv_weight, preferred_element_type=jnp.float32
    ).astype(jnp.bfloat16)
    query_rows = qkv[0].reshape(seq_rows, head_count, head_size)
    key_rows = qkv[1].reshape(seq_rows, head_count, head_size)
    value_rows = qkv[2].reshape(seq_rows, head_count, head_size)
    bucket_table = (
        buckets[:, None] == lax.broadcasted_iota(jnp.int32, (buckets.shape[0], bucket_count), 1)
    ).astype(jnp.float32)
    dist_bias = jnp.dot(bucket_table, rel_bias, precision=lax.Precision.HIGHEST).T

    def scores_of(row_start):
        query_block = query_rows[row_start : row_start + block_rows]
        raw_scores = jnp.einsum(
            "qhe,khe->hqk", query_block, key_rows, preferred_element_type=jnp.float32
        )
        bias_rows = skew_bias(dist_bias, row_start, block_rows, seq_rows)
        same_doc = seg_row[row_start : row_start + block_rows, None] == seg_row[None, :]
        return (jnp.where(same_doc[None], raw_scores + bias_rows, negative), query_block)

    context_blocks = []
    log_totals = []
    for row_start in row_starts:
        scores, query_block = scores_of(row_start)
        row_max = jnp.max(scores, axis=2, keepdims=True)
        exp_scores = jnp.exp(scores - row_max)
        row_total = jnp.sum(exp_scores, axis=2, keepdims=True)
        attn_probs = (exp_scores / row_total).astype(jnp.bfloat16)
        context_blocks.append(
            jnp.einsum(
                "hqk,khe->qhe", attn_probs, value_rows, preferred_element_type=jnp.float32
            ).reshape(block_rows, columns)
        )
        log_totals.append(row_max + jnp.log(row_total))
    context = jnp.concatenate(context_blocks, axis=0).astype(jnp.bfloat16)
    picked = context
    attn_out = lax.psum_scatter(
        jnp.dot(picked, out_weight, preferred_element_type=jnp.float32),
        "tensor",
        scatter_dimension=0,
        tiled=True,
    )
    h_one = inputs_f32 + attn_out
    normed_moe = rms_apply(h_one, norm_moe).astype(jnp.bfloat16)
    logits = jnp.dot(normed_moe, router_weight, preferred_element_type=jnp.float32)
    router_probs = jax.nn.softmax(logits, axis=-1)
    picked_mine = route_mine[:, None] == lax.broadcasted_iota(
        jnp.int32, (own_rows, expert_count), 1
    )
    gate_value = jnp.sum(jnp.where(picked_mine, router_probs, 0.0), axis=1)
    chosen = route_seq[:, None] == lax.broadcasted_iota(jnp.int32, (seq_rows, expert_count), 1)
    running = jnp.cumsum(chosen.astype(jnp.int32), axis=0)
    slot_index = jnp.sum(jnp.where(chosen, running - 1, 0), axis=1)
    position = route_seq * capacity + slot_index
    dispatch = (
        lax.broadcasted_iota(jnp.int32, (slot_total, seq_rows), 0) == position[None, :]
    ).astype(jnp.bfloat16)

    def add_rows(incoming):
        return jnp.dot(dispatch, incoming, preferred_element_type=jnp.float32)

    slot_rows = add_rows(lax.all_gather(normed_moe, "tensor", axis=0, tiled=True))
    slot_rows = slot_rows.astype(jnp.bfloat16).reshape(expert_count, capacity, width_model)
    expert_inputs = lax.all_to_all(slot_rows, "dp", split_axis=0, concat_axis=1, tiled=True)
    pre_act = jnp.einsum(
        "erd,edf->erf", expert_inputs, expert_in, preferred_element_type=jnp.float32
    )
    act_value, act_back = jax.vjp(smooth_act, pre_act)
    hidden = act_value.astype(jnp.bfloat16)
    expert_part = jnp.einsum(
        "erf,efd->erd", hidden, expert_out, preferred_element_type=jnp.float32
    ).astype(jnp.bfloat16)
    expert_sum = to_tokens(expert_part, dispatch)
    output = (h_one + gate_value[:, None] * expert_sum).astype(jnp.bfloat16)
    grad_out = cotangent.astype(jnp.float32)
    grad_gate = jnp.sum(grad_out * expert_sum, axis=1)
    grad_expert_sum = (gate_value[:, None] * grad_out).astype(jnp.bfloat16)
    grad_slots = add_rows(lax.all_gather(grad_expert_sum, "tensor", axis=0, tiled=True))
    grad_slots = grad_slots.astype(jnp.bfloat16).reshape(expert_count, capacity, width_model)
    grad_part = lax.all_to_all(grad_slots, "dp", split_axis=0, concat_axis=1, tiled=True)
    grad_expert_out = jnp.einsum(
        "erf,erd->efd", hidden, grad_part, preferred_element_type=jnp.float32
    )
    grad_hidden = jnp.einsum(
        "erd,efd->erf", grad_part, expert_out, preferred_element_type=jnp.float32
    )
    grad_pre = act_back(grad_hidden)[0].astype(jnp.bfloat16)
    grad_expert_in = jnp.einsum(
        "erd,erf->edf", expert_inputs, grad_pre, preferred_element_type=jnp.float32
    )
    grad_rows_part = jnp.einsum(
        "erf,edf->erd", grad_pre, expert_in, preferred_element_type=jnp.float32
    ).astype(jnp.bfloat16)
    grad_normed_moe = to_tokens(grad_rows_part, dispatch)
    grad_logits = (
        gate_value[:, None] * grad_gate[:, None] * (picked_mine.astype(jnp.float32) - router_probs)
    ).astype(jnp.bfloat16)
    grad_router = lax.dot_general(
        normed_moe, grad_logits, (((0,), (0,)), ((), ())), preferred_element_type=jnp.float32
    )
    grad_normed_moe = grad_normed_moe + lax.dot_general(
        grad_logits, router_weight, (((1,), (1,)), ((), ())), preferred_element_type=jnp.float32
    )
    moe_norm_out, moe_norm_back = jax.vjp(rms_apply, h_one, norm_moe)
    grad_h_norm, grad_norm_moe = moe_norm_back(grad_normed_moe)
    grad_h_one = grad_out + grad_h_norm
    grad_attn_rows = lax.all_gather(grad_h_one.astype(jnp.bfloat16), "tensor", axis=0, tiled=True)
    grad_out_weight = lax.dot_general(
        context, grad_attn_rows, (((0,), (0,)), ((), ())), preferred_element_type=jnp.float32
    )
    grad_context = lax.dot_general(
        grad_attn_rows, out_weight, (((1,), (1,)), ((), ())), preferred_element_type=jnp.float32
    ).astype(jnp.bfloat16)
    grad_query_blocks = []
    grad_key = jnp.zeros((seq_rows, head_count, head_size), jnp.float32)
    grad_value = jnp.zeros((seq_rows, head_count, head_size), jnp.float32)
    grad_dist = jnp.zeros((head_count, 2 * seq_rows - 1), jnp.float32)
    for block_number, row_start in enumerate(row_starts):
        scores, query_block = scores_of(row_start)
        attn_probs = jnp.exp(scores - log_totals[block_number])
        grad_block = grad_context[row_start : row_start + block_rows].reshape(
            block_rows, head_count, head_size
        )
        grad_probs = jnp.einsum(
            "qhe,khe->hqk", grad_block, value_rows, preferred_element_type=jnp.float32
        )
        row_delta = jnp.sum(attn_probs * grad_probs, axis=2, keepdims=True)
        grad_scores = (attn_probs * (grad_probs - row_delta)).astype(jnp.bfloat16)
        grad_query_blocks.append(
            jnp.einsum("hqk,khe->qhe", grad_scores, key_rows, preferred_element_type=jnp.float32)
        )
        grad_key = grad_key + jnp.einsum(
            "hqk,qhe->khe", grad_scores, query_block, preferred_element_type=jnp.float32
        )
        grad_value = grad_value + jnp.einsum(
            "hqk,qhe->khe",
            attn_probs.astype(jnp.bfloat16),
            grad_block,
            preferred_element_type=jnp.float32,
        )
        grad_dist = grad_dist + skew_back(
            grad_scores.astype(jnp.float32), row_start, block_rows, seq_rows
        )
    grad_query = jnp.concatenate(grad_query_blocks, axis=0)
    grad_qkv = (
        jnp.stack([grad_query, grad_key, grad_value])
        .reshape(3, seq_rows, columns)
        .astype(jnp.bfloat16)
    )
    grad_qkv_weight = jnp.einsum(
        "sd,csf->cdf", seq_normed, grad_qkv, preferred_element_type=jnp.float32
    )
    picked = grad_qkv
    grad_normed_attn = lax.psum_scatter(
        jnp.einsum("csf,cdf->sd", picked, qkv_weight, preferred_element_type=jnp.float32),
        "tensor",
        scatter_dimension=0,
        tiled=True,
    )
    attn_norm_out, attn_norm_back = jax.vjp(rms_apply, inputs_f32, norm_attn)
    grad_in_norm, grad_norm_attn = attn_norm_back(grad_normed_attn)
    grad_inputs = grad_h_one + grad_in_norm
    grad_rel_bias = jnp.dot(bucket_table.T, grad_dist.T, precision=lax.Precision.HIGHEST)
    summed_layer = lax.psum((grad_qkv_weight, grad_out_weight, grad_rel_bias), "dp")
    summed_shared = lax.psum((grad_norm_attn, grad_norm_moe, grad_router), ("dp", "tensor"))
    return (
        output,
        grad_inputs,
        summed_layer[0],
        summed_layer[1],
        summed_layer[2],
        summed_shared[0],
        summed_shared[1],
        summed_shared[2],
        grad_expert_in,
        grad_expert_out,
    )


def solution(mesh):
    placed = (
        P(("dp", "tensor"), None),
        P("dp", None),
        P(),
        P("dp", None, None),
        P(None, None, "tensor"),
        P("tensor", None),
        P(None, "tensor"),
        P(),
        P(),
        P(),
        P("dp", None, "tensor"),
        P("dp", "tensor", None),
        P(("dp", "tensor"), None),
    )
    return jax.shard_map(
        per_device,
        mesh=mesh,
        in_specs=placed,
        out_specs=(
            P(("dp", "tensor"), None),
            P(("dp", "tensor"), None),
            P(None, None, "tensor"),
            P("tensor", None),
            P(None, "tensor"),
            P(),
            P(),
            P(),
            P("dp", None, "tensor"),
            P("dp", "tensor", None),
        ),
        check_vma=False,
    )
```

profile of v0, /device:TPU:10, one launch (start us, length us, event | category | flops | bytes accessed | tf_op | source)
XLA Modules:
  0.0 811.8 jit_solution(8059519370671081679)
XLA Ops:
  13.0 4.8 tile.10
  17.9 15.5 %reshape.287 = f32[2357760]{0:T(1024)} reshape(f32[3,512,1535]{2,1,0:T(8,128)} %tile.10) | data formatting | bytes 18862080
  33.3 13.2 %tile.11 = f32[3,785920]{1,0:T(4,128)} reshape(f32[2357760]{0:T(1024)} %reshape.287) | data formatting | bytes 18862080 | tf_op jit(solution)/shard_map/tile | solution.py:24
  46.5 13.6 %slice.95 = f32[3,785408]{1,0:T(4,128)} slice(f32[3,785920]{1,0:T(4,128)} %tile.11), slice={[0:3], [511:785919]} | slice | bytes 18849792 | tf_op jit(solution)/shard_map/slice | solution.py:25
  60.1 13.2 %reshape.289 = f32[2356224]{0:T(1024)} reshape(f32[3,785408]{1,0:T(4,128)} %slice.95) | data formatting | bytes 18849792
  73.3 10.9 %reshape.262 = f32[3,512,1534]{2,1,0:T(8,128)} reshape(f32[2356224]{0:T(1024)} %reshape.289) | data formatting | bytes 18849792 | tf_op jit(solution)/shard_map/reshape | solution.py:26
  84.2 4.8 tile.8
  89.0 15.6 %reshape.291 = f32[2357760]{0:T(1024)} reshape(f32[3,512,1535]{2,1,0:T(8,128)} %tile.8) | data formatting | bytes 18862080
  104.6 13.2 %tile.9 = f32[3,785920]{1,0:T(4,128)} reshape(f32[2357760]{0:T(1024)} %reshape.291) | data formatting | bytes 18862080 | tf_op jit(solution)/shard_map/tile | solution.py:24
  117.8 13.5 %slice.91 = f32[3,785408]{1,0:T(4,128)} slice(f32[3,785920]{1,0:T(4,128)} %tile.9), slice={[0:3], [511:785919]} | slice | bytes 18849792 | tf_op jit(solution)/shard_map/slice | solution.py:25
  131.3 13.3 %reshape.293 = f32[2356224]{0:T(1024)} reshape(f32[3,785408]{1,0:T(4,128)} %slice.91) | data formatting | bytes 18849792
  144.6 11.0 %reshape.260 = f32[3,512,1534]{2,1,0:T(8,128)} reshape(f32[2356224]{0:T(1024)} %reshape.293) | data formatting | bytes 18849792 | tf_op jit(solution)/shard_map/reshape | solution.py:26
  157.0 2.8 fusion.91
  160.8 4.2 fusion.88
  176.4 2.3 fusion.64
  178.8 38.3 %reduce-scatter.5.cloned.1.call-done = f32[256,768]{1,0:T(8,128)} async-done(((f32[1024,768]{1,0:T(8,128)}), f32[256,768]{1,0:T(8,128)}) %reduce-scatter.5.cloned.1.call-update) | async-done | bytes 786448 | tf_op jit(solution)/shard_map/reduce_scatter | solution.py:124
  221.2 9.3 %reduce-window.6 = s32[16,8,128]{2,1,0:T(8,128)} reduce-window(s32[16,8,128]{2,1,0:T(8,128)} %fusion.67, s32[]{:T(128)} %constant.16.clone.1), window={size=1x1x128 pad=0_0x0_0x127_0}, to_apply=%region_10.11 | reduce-window | flops 2080768 | bytes 131076 | tf_op jit(solution)/shard_map/reduce-window
  234.2 6.2 all-gather.7.cloned.1.call-done
  240.4 3.8 fusion.17
  244.2 51.4 %all_to_all.66 = bf16[16,80,768]{2,1,0:T(8,128)(2,1)S(1)} all-to-all(bf16[16,80,768]{2,1,0:T(8,128)(2,1)S(1)} %bitcast.150), channel_id=1, replica_groups=mesh['dp'=8,'tensor'=4] {'dp'}, dimensions={0} | all-to-all | bytes 3932160 | tf_op jit(solution)/shard_map/all_to_all | solution.py:151
  298.9 1.9 copy-done.75
  300.8 1.9 convolution_convert_fusion.1
  302.7 2.0 copy.48
  304.8 48.7 %all_to_all.67 = bf16[2,640,768]{2,0,1:T(2,128)(2,1)S(1)} all-to-all(bf16[2,640,768]{2,0,1:T(2,128)(2,1)S(1)} %copy.48), channel_id=1, replica_groups=mesh['dp'=8,'tensor'=4] {'dp'}, dimensions={1} | all-to-all | bytes 3932160 | tf_op jit(solution)/shard_map/all_to_all | solution.py:47
  353.8 3.7 fusion.31
  360.1 24.1 %reduce-scatter.7.cloned.1.call-done = bf16[256,768]{1,0:T(8,128)(2,1)} async-done(((bf16[1024,768]{1,0:T(8,128)(2,1)}), bf16[256,768]{1,0:T(8,128)(2,1)}) %reduce-scatter.7.cloned.1.call-update) | async-done | bytes 393232 | tf_op jit(solution)/shard_map/reduce_scatter | solution.py:49
  384.1 2.6 fusion.57
  386.8 19.8 %all-gather.9.cloned.1.call-done = bf16[1024,768]{1,0:T(8,128)(2,1)} async-done(((bf16[256,768]{1,0:T(8,128)(2,1)}), bf16[1024,768]{1,0:T(8,128)(2,1)}) %all-gather.9.cloned.1.call-update) | async-done | bytes 1572880 | tf_op jit(solution)/shard_map/all_gather | solution.py:165
  406.6 3.8 fusion.18
  410.5 51.3 %all_to_all.68 = bf16[16,80,768]{2,1,0:T(8,128)(2,1)S(1)} all-to-all(bf16[16,80,768]{2,1,0:T(8,128)(2,1)S(1)} %bitcast.152), channel_id=1, replica_groups=mesh['dp'=8,'tensor'=4] {'dp'}, dimensions={0} | all-to-all | bytes 3932160 | tf_op jit(solution)/shard_map/all_to_all | solution.py:167
  462.0 3.7 fusion.16
  467.4 2.0 copy.52
  469.5 48.7 %all_to_all.69 = bf16[2,640,768]{2,0,1:T(2,128)(2,1)S(1)} all-to-all(bf16[2,640,768]{2,0,1:T(2,128)(2,1)S(1)} %copy.52), channel_id=1, replica_groups=mesh['dp'=8,'tensor'=4] {'dp'}, dimensions={1} | all-to-all | bytes 3932160 | tf_op jit(solution)/shard_map/all_to_all | solution.py:47
  518.9 3.7 fusion.32
  522.7 26.5 %reduce-scatter.9.cloned.1.call-done = bf16[256,768]{1,0:T(8,128)(2,1)} async-done(((bf16[1024,768]{1,0:T(8,128)(2,1)}), bf16[256,768]{1,0:T(8,128)(2,1)}) %reduce-scatter.9.cloned.1.call-update) | async-done | bytes 393232 | tf_op jit(solution)/shard_map/reduce_scatter | solution.py:49
  549.3 2.1 multiply_reduce_fusion.2
  554.8 6.5 fusion.94
  561.3 4.6 fusion.82
  566.0 6.3 all-gather.11.cloned.1.call-done
  572.3 2.1 convolution_convert_fusion.2
  574.4 4.1 fusion.19
  578.5 4.2 multiply_reduce_fusion
  582.8 1.9 multiply_reduce_fusion.1
  594.6 3.2 convolution_bitcast_fusion.1
  597.8 4.4 pad.29
  602.2 10.2 %reshape.295 = bf16[2356224]{0:T(1024)(128)(2,1)} reshape(bf16[3,512,1534]{2,1,0:T(8,128)(2,1)} %pad.29) | data formatting | bytes 9424896
  612.4 6.8 reshape.274
  619.2 10.0 %pad_convert_fusion = f32[3,785920]{1,0:T(4,128)} fusion(bf16[3,785408]{1,0:T(4,128)(2,1)} %reshape.274), kind=kLoop, calls=%fused_computation.14 | loop fusion | flops 2357760 | bytes 14143488 | tf_op jit(solution)/shard_map/reshape | solution.py:36
  629.2 2.5 pad.26
  631.7 9.7 %reshape.299 = bf16[2356224]{0:T(1024)(128)(2,1)} reshape(bf16[3,512,1534]{2,1,0:T(8,128)(2,1)} %pad.26) | data formatting | bytes 9424896
  641.4 7.1 reshape.271
  649.8 3.8 fusion.35
  653.7 10.1 %pad_convert_fusion.1 = f32[3,785920]{1,0:T(4,128)} fusion(bf16[3,785408]{1,0:T(4,128)(2,1)} %reshape.271), kind=kLoop, calls=%fused_computation.15 | loop fusion | flops 2357760 | bytes 14143488 | tf_op jit(solution)/shard_map/reshape | solution.py:36
  663.8 13.2 %reshape.297 = f32[2357760]{0:T(1024)} reshape(f32[3,785920]{1,0:T(4,128)} %pad_convert_fusion) | data formatting | bytes 18862080
  677.0 15.9 %reshape.280 = f32[3,512,1535]{2,1,0:T(8,128)} reshape(f32[2357760]{0:T(1024)} %reshape.297) | data formatting | bytes 18862080 | tf_op jit(solution)/shard_map/reshape | solution.py:36
  692.9 13.4 %reshape.301 = f32[2357760]{0:T(1024)} reshape(f32[3,785920]{1,0:T(4,128)} %pad_convert_fusion.1) | data formatting | bytes 18862080
  706.3 15.9 %reshape.278 = f32[3,512,1535]{2,1,0:T(8,128)} reshape(f32[2357760]{0:T(1024)} %reshape.301) | data formatting | bytes 18862080 | tf_op jit(solution)/shard_map/reshape | solution.py:36
  722.1 4.2 reduce_sum.181
  726.5 4.3 reduce_sum.180
  731.4 19.6 %psum.44 = f32[32,3]{0,1:T(4,128)} all-reduce(f32[32,3]{0,1:T(4,128)S(1)} %fusion.49), channel_id=1, replica_groups=mesh['dp'=8,'tensor'=4] {'dp'}, use_global_device_ids=true, to_apply=%region_25.26 | all-reduce | flops 96 | bytes 768 | tf_op jit(solution)/shard_map/psum | solution.py:251
  751.0 2.0 fusion.53
  753.0 44.2 %all-reduce.6 = (f32[768]{0:T(1024)}, f32[768]{0:T(1024)}, f32[768,16]{0,1:T(8,128)}) all-reduce(f32[768]{0:T(1024)S(1)} %get-tuple-element.12, f32[768]{0:T(1024)S(1)} %copy-done.56, f32[768,16]{0,1:T(8,128)S(1)} %copy-done.32), channel_id=1, replica_groups=mesh['dp'=8,'tensor'=4] {'dp','tensor'}, use_global_device_ids=true, to_apply=%region_27.28 | all-reduce | flops 13824 | bytes 110592 | tf_op jit(solution)/shard_map/psum | solution.py:252
  798.0 3.1 fusion.58
  801.1 2.9 copy.63
  (251 shorter events, 52.9 us)
Async XLA Ops:
  7.2 293.6 %copy-start = (bf16[2,768,768]{2,1,0:T(8,128)(2,1)S(1)}, bf16[2,768,768]{2,1,0:T(8,128)(2,1)}, u32[]{:S(2)}) copy-start(bf16[2,768,768]{2,1,0:T(8,128)(2,1)} %param.24) | copy-start | bytes 7077892
  7.2 149.8 %all-gather.5.cloned.1.call-start = ((), (), s32[]{:S(2)}) async-start(), calls=%async_computation.8 | async-start | bytes 1966080 | tf_op jit(solution)/shard_map/all_gather | solution.py:87
  11.5 205.5 %reduce-scatter.5.cloned.1.call-start = ((), (), s32[]{:S(2)}) async-start(), calls=%async_computation.9 | async-start | bytes 3932160 | tf_op jit(solution)/shard_map/reduce_scatter | solution.py:124
  144.6 11.0 %copy-start.62 = (s32[1,1024]{1,0:T(1,128)S(1)}, s32[1,1024]{1,0:T(1,128)}, u32[]{:S(2)}) copy-start(s32[1,1024]{1,0:T(1,128)} %param.14) | copy-start | bytes 12292
  160.0 14.0 %copy-start.10 = (bf16[1,1024,192]{1,2,0:T(8,128)(2,1)}, bf16[1,1024,192]{1,2,0:T(8,128)(2,1)S(1)}, u32[]{:S(2)}) copy-start(bf16[1,1024,192]{1,2,0:T(8,128)(2,1)S(1)} %get-tuple-element.24) | copy-start | bytes 1179652
  160.0 4.9 copy-start.13
  160.0 8.4 %copy-start.19 = (bf16[1,512,192]{1,2,0:T(8,128)(2,1)}, bf16[1,512,192]{1,2,0:T(8,128)(2,1)S(1)}, u32[]{:S(2)}) copy-start(bf16[1,512,192]{1,2,0:T(8,128)(2,1)S(1)} %get-tuple-element.21) | copy-start | bytes 589828
  166.5 4.1 slice-start.5
  166.5 4.3 slice-start.6
  168.5 7.3 copy-start.22
  176.4 43.2 %copy-start.40 = (f32[768]{0:T(1024)S(1)}, f32[768]{0:T(1024)}, u32[]{:S(2)}) copy-start(f32[768]{0:T(1024)} %param.21) | copy-start | bytes 9220
  178.7 41.9 %copy-start.43 = (s32[1,1024,1]{1,2,0:T(1,128)S(1)}, s32[1,1024,1]{1,2,0:T(1,128)}, u32[]{:S(2)}) copy-start(s32[1,1024,1]{1,2,0:T(1,128)} %param.16) | copy-start | bytes 12292
  178.7 61.7 %all-gather.7.cloned.1.call-start = ((), (), s32[]{:S(2)}) async-start(), calls=%async_computation.10 | async-start | bytes 1966080 | tf_op jit(solution)/shard_map/all_gather | solution.py:149
  220.6 163.6 %reduce-scatter.7.cloned.1.call-start = ((), (), s32[]{:S(2)}) async-start(), calls=%async_computation.11 | async-start | bytes 1966080 | tf_op jit(solution)/shard_map/reduce_scatter | solution.py:49
  234.2 119.6 %copy-start.68 = (s32[1024]{0:T(1024)}, s32[1024]{0:T(1024)S(1)}, u32[]{:S(2)}) copy-start(s32[1024]{0:T(1024)S(1)} %multiply_add_fusion) | copy-start | bytes 12292
  244.2 52.9 %copy-start.70 = (bf16[2,768,768]{2,1,0:T(8,128)(2,1)S(1)}, bf16[2,768,768]{2,1,0:T(8,128)(2,1)}, u32[]{:S(2)}) copy-start(bf16[2,768,768]{2,1,0:T(8,128)(2,1)} %param.23) | copy-start | bytes 7077892
  357.5 49.1 %all-gather.9.cloned.1.call-start = ((), (), s32[]{:S(2)}) async-start(), calls=%async_computation.12 | async-start | bytes 1966080 | tf_op jit(solution)/shard_map/all_gather | solution.py:165
  386.8 162.5 %reduce-scatter.9.cloned.1.call-start = ((), (), s32[]{:S(2)}) async-start(), calls=%async_computation.13 | async-start | bytes 1966080 | tf_op jit(solution)/shard_map/reduce_scatter | solution.py:49
  410.4 51.5 %copy-start.76 = (f32[2,640,768]{2,1,0:T(8,128)S(1)}, f32[2,640,768]{2,1,0:T(8,128)}, u32[]{:S(2)}) copy-start(f32[2,640,768]{2,1,0:T(8,128)} %copy-done.75) | copy-start | bytes 11796484
  461.9 3.8 copy-start.17
  461.9 3.7 copy-start.71
  518.8 3.9 copy-start.57
  518.8 3.9 copy-start.67
  518.8 30.4 %copy-start.35 = (bf16[768,16]{0,1:T(8,128)(2,1)S(1)}, bf16[768,16]{0,1:T(8,128)(2,1)}, u32[]{:S(2)}) copy-start(bf16[768,16]{0,1:T(8,128)(2,1)} %param.22) | copy-start | bytes 73732
  518.8 30.4 %copy-start.41 = (f32[768]{0:T(1024)S(1)}, f32[768]{0:T(1024)}, u32[]{:S(2)}) copy-start(f32[768]{0:T(1024)} %param.21) | copy-start | bytes 9220
  518.9 30.4 %copy-start.50 = (f32[256]{0:T(256)S(1)}, f32[256]{0:T(256)}, u32[]{:S(2)}) copy-start(f32[256]{0:T(256)} %copy-done.49) | copy-start | bytes 3076
  518.9 30.4 %copy-start.52 = (f32[256]{0:T(256)S(1)}, f32[256]{0:T(256)}, u32[]{:S(2)}) copy-start(f32[256]{0:T(256)} %copy-done.51) | copy-start | bytes 3076
  518.9 30.4 %copy-start.59 = (f32[256]{0:T(256)S(1)}, f32[256]{0:T(256)}, u32[]{:S(2)}) copy-start(f32[256]{0:T(256)} %copy-done.58) | copy-start | bytes 3076
  518.9 30.4 %copy-start.61 = (s32[1,256,1]{1,2,0:T(1,128)S(1)}, s32[1,256,1]{1,2,0:T(1,128)}, u32[]{:S(2)}) copy-start(s32[1,256,1]{1,2,0:T(1,128)} %copy-done.60) | copy-start | bytes 3076
  518.9 32.5 %copy-start.64 = (f32[256]{0:T(256)S(1)}, f32[256]{0:T(256)}, u32[]{:S(2)}) copy-start(f32[256]{0:T(256)} %copy-done.63) | copy-start | bytes 3076
  518.9 32.5 %copy-start.12 = (bf16[256,768]{1,0:T(8,128)(2,1)S(1)}, bf16[256,768]{1,0:T(8,128)(2,1)}, u32[]{:S(2)}) copy-start(bf16[256,768]{1,0:T(8,128)(2,1)} %param.25) | copy-start | bytes 1179652
  522.6 30.1 %copy-start.37 = (f32[3,512]{1,0:T(4,128)S(1)}, f32[3,512]{1,0:T(4,128)}, u32[]{:S(2)}) copy-start(f32[3,512]{1,0:T(4,128)} %copy-done.36) | copy-start | bytes 18436
  522.6 30.1 %copy-start.46 = (f32[3,512]{1,0:T(4,128)S(1)}, f32[3,512]{1,0:T(4,128)}, u32[]{:S(2)}) copy-start(f32[3,512]{1,0:T(4,128)} %copy-done.45) | copy-start | bytes 18436
  522.6 30.7 %copy-start.39 = (f32[3,512]{1,0:T(4,128)S(1)}, f32[3,512]{1,0:T(4,128)}, u32[]{:S(2)}) copy-start(f32[3,512]{1,0:T(4,128)} %copy-done.38) | copy-start | bytes 18436
  522.6 30.7 %copy-start.48 = (f32[3,512]{1,0:T(4,128)S(1)}, f32[3,512]{1,0:T(4,128)}, u32[]{:S(2)}) copy-start(f32[3,512]{1,0:T(4,128)} %copy-done.47) | copy-start | bytes 18436
  522.6 31.4 %copy-start.9 = (bf16[256,768]{1,0:T(8,128)(2,1)S(1)}, bf16[256,768]{1,0:T(8,128)(2,1)}, u32[]{:S(2)}) copy-start(bf16[256,768]{1,0:T(8,128)(2,1)} %multiply_convert_fusion.3) | copy-start | bytes 1179652
  522.7 49.6 %all-gather.11.cloned.1.call-start = ((), (), s32[]{:S(2)}) async-start(), calls=%async_computation.14 | async-start | bytes 1966080 | tf_op jit(solution)/shard_map/all_gather | solution.py:194
  551.4 9.9 %copy-start.8 = (f32[256,768]{1,0:T(8,128)}, f32[256,768]{1,0:T(8,128)S(1)}, u32[]{:S(2)}) copy-start(f32[256,768]{1,0:T(8,128)S(1)} %get-tuple-element.43) | copy-start | bytes 2359300
  551.4 9.9 %copy-start.65 = (f32[256]{0:T(256)}, f32[256]{0:T(256)S(1)}, u32[]{:S(2)}) copy-start(f32[256]{0:T(256)S(1)} %multiply_multiply_fusion.3) | copy-start | bytes 3076
  552.5 198.5 %reduce-scatter.11.cloned.1.call-start = ((), (), s32[]{:S(2)}) async-start(), calls=%async_computation.15 | async-start | bytes 3932160 | tf_op jit(solution)/shard_map/reduce_scatter | solution.py:241
  554.8 6.5 copy-start.18
  554.8 6.5 copy-start.77
  561.3 11.0 %copy-start.31 = (bf16[192,768]{1,0:T(8,128)(2,1)S(1)}, bf16[192,768]{1,0:T(8,128)(2,1)}, u32[]{:S(2)}) copy-start(bf16[192,768]{1,0:T(8,128)(2,1)} %param.18) | copy-start | bytes 884740
  561.3 13.1 %copy-start.34 = (f32[3,512]{1,0:T(4,128)S(1)}, f32[3,512]{1,0:T(4,128)}, u32[]{:S(2)}) copy-start(f32[3,512]{1,0:T(4,128)} %log_add_fusion) | copy-start | bytes 18436
  574.3 4.2 copy-start.11
  574.4 8.3 %slice-start = ((s8[6291456]{0:T(1024)(128)(4,1)}), s8[4194304]{0:T(1024)(128)(4,1)S(1)}, s32[]{:S(2)}) async-start(s8[6291456]{0:T(1024)(128)(4,1)} %bitcast.124), calls=%async_computation.17 | async-start | bytes 8388608
  578.5 4.2 slice-start.1
  578.5 4.2 copy-start.33
  590.1 4.1 copy-start.27
  597.8 203.4 %all-reduce.10.cloned.1.call-start = ((), (), s32[]{:S(2)}) async-start(), calls=%async_computation.16 | async-start | bytes 4718592 | tf_op jit(solution)/shard_map/psum | solution.py:251
  619.2 10.0 %copy-start.6 = (bf16[3,512,1024]{2,1,0:T(8,128)(2,1)S(1)}, bf16[3,512,1024]{2,1,0:T(8,128)(2,1)}, u32[]{:S(2)}) copy-start(bf16[3,512,1024]{2,1,0:T(8,128)(2,1)} %copy-done.5) | copy-start | bytes 9437188
  641.4 7.1 copy-start.21
  641.4 7.1 copy-start.23
  641.4 7.1 copy-start.25
  641.4 8.4 %copy-start.28 = (bf16[3,64,1024]{2,1,0:T(8,128)(2,1)S(1)}, bf16[3,64,1024]{2,1,0:T(8,128)(2,1)}, u32[]{:S(2)}) copy-start(bf16[3,64,1024]{2,1,0:T(8,128)(2,1)} %copy-done.27) | copy-start | bytes 1179652
  726.4 4.4 copy-start.73
  726.4 24.6 %copy-start.7 = (bf16[256,768]{1,0:T(8,128)(2,1)S(1)}, bf16[256,768]{1,0:T(8,128)(2,1)}, u32[]{:S(2)}) copy-start(bf16[256,768]{1,0:T(8,128)(2,1)} %param.13) | copy-start | bytes 1179652
  726.4 24.6 %copy-start.44 = (f32[768]{0:T(1024)S(1)}, f32[768]{0:T(1024)}, u32[]{:S(2)}) copy-start(f32[768]{0:T(1024)} %param.20) | copy-start | bytes 9220
  726.4 24.6 %copy-start.55 = (f32[256]{0:T(256)S(1)}, f32[256]{0:T(256)}, u32[]{:S(2)}) copy-start(f32[256]{0:T(256)} %copy-done.54) | copy-start | bytes 3076
  726.4 26.5 %copy-start.32 = (f32[768,16]{0,1:T(8,128)S(1)}, f32[768,16]{0,1:T(8,128)}, u32[]{:S(2)}) copy-start(f32[768,16]{0,1:T(8,128)} %fusion.80) | copy-start | bytes 147460
  726.5 26.5 %copy-start.56 = (f32[768]{0:T(1024)S(1)}, f32[768]{0:T(1024)}, u32[]{:S(2)}) copy-start(f32[768]{0:T(1024)} %get-tuple-element.10) | copy-start | bytes 9220
  726.5 71.5 %copy-start.42 = (f32[768]{0:T(1024)S(1)}, f32[768]{0:T(1024)}, u32[]{:S(2)}) copy-start(f32[768]{0:T(1024)} %param.21) | copy-start | bytes 9220
  726.5 71.5 %copy-start.53 = (f32[256]{0:T(256)S(1)}, f32[256]{0:T(256)}, u32[]{:S(2)}) copy-start(f32[256]{0:T(256)} %copy-done.51) | copy-start | bytes 3076
  797.2 7.6 copy-start.1
  (30 other events, 53.7 us)
Sparse Core Ops, SparseCore 0:
  11.7 19.8 all-gather.4
  178.8 38.1 reduce-scatter.4
  220.7 19.6 all-gather.6
  357.7 26.4 reduce-scatter.6
  386.9 19.6 all-gather.8
  522.8 26.4 reduce-scatter.8
  552.6 19.6 all-gather.10
  597.9 37.9 reduce-scatter.10
  653.8 109.6 all-reduce.9
where the time goes:
time: 824 us; the launch traced here: 812 us
  local copies, waits for them, and re-layouts  266 us (32%)
  blocking collectives  264 us (32%)
  waiting for transfers between devices  121 us (15%)
  matrix products  81.1 us (10%)
  other arithmetic  63.8 us (8%)
  between operations  15.4 us (2%)
    unnamed x180, local copies, waits for them, and re-layouts  120 us
    all_to_all x2, blocking collectives, to_tokens(): lax.all_to_all(expert_buffer, 'dp', split_axis=1, concat_axis=0, tiled=True)  97.3 us
    all_to_all x1, blocking collectives, per_device(): lax.all_to_all(slot_rows, 'dp', split_axis=0, concat_axis=1, tiled=True)  51.4 us
    all_to_all x1, blocking collectives, per_device(): lax.all_to_all(grad_slots, 'dp', split_axis=0, concat_axis=1, tiled=True)  51.3 us
    reduce_scatter x2, waiting for transfers between devices, to_tokens(): lax.psum_scatter(rows_of(dispatch, returned).astype(jnp.bfloat16), 'tenso...  50.6 us
    psum x1, blocking collectives, per_device(): lax.psum((grad_norm_attn, grad_norm_moe, grad_router), ('dp', 'tensor'))  44.2 us
    reduce_scatter x1, waiting for transfers between devices, per_device(): lax.psum_scatter(jnp.dot(picked, out_weight, preferred_element_type=jnp.f...  38.3 us
    another operation x4, local copies, waits for them, and re-layouts, skew_bias(): tiled = jnp.tile(window, (1, block_rows))  36 us
  transfers between devices with their start and end apart: 9, of which 6 were waited for; matrix products, arithmetic and copies ran while one was open for 39% of the time, Pallas kernels for 0%

commit v1 on v0

v1 whole, which is shorter than its diff:
```python
import functools

import jax
import jax.numpy as jnp
from jax import lax
from jax.experimental import pallas as pl
from jax.experimental.pallas import tpu as pltpu
from jax.sharding import PartitionSpec as P

epsilon = 1e-06
negative = -1000000000.0
bf16 = jnp.bfloat16
f32 = jnp.float32
reach = 256
rows_q = 128
window = rows_q + 2 * reach
table = window + rows_q
head_size = 64
mega = 1024 * 1024

core_pairs = [(0, 1), (1, 0), (2, 3), (3, 2)]
x_pairs = [(0, 2), (2, 0), (1, 3), (3, 1)]


def core_hop(value):
    return lax.ppermute(value, "tensor", core_pairs)


def x_hop(value):
    return lax.ppermute(value, "tensor", x_pairs)


def gather4(value):
    other = x_hop(value)
    return value, core_hop(value), other, core_hop(other)


def dot(a, b, dims):
    return lax.dot_general(a, b, (dims, ((), ())), preferred_element_type=f32)


def mm(a, b):
    return dot(a, b, ((1,), (0,)))


def mm_nt(a, b):
    return dot(a, b, ((1,), (1,)))


def mm_tn(a, b):
    return dot(a, b, ((0,), (0,)))


def shape(dims, kind):
    return jax.ShapeDtypeStruct(dims, kind)


def run(body, outs, args, smem=(), scratch=(), limit=48, flops=0, name=None):
    specs = [
        pl.BlockSpec(memory_space=pltpu.SMEM if i in smem else pltpu.VMEM)
        for i in range(len(args))
    ]
    moved = sum(a.size * a.dtype.itemsize for a in args) + sum(
        o.size * jnp.dtype(o.dtype).itemsize for o in outs
    )
    return pl.pallas_call(
        body,
        out_shape=outs,
        in_specs=specs,
        out_specs=[pl.BlockSpec(memory_space=pltpu.VMEM)] * len(outs),
        scratch_shapes=list(scratch),
        compiler_params=pltpu.CompilerParams(vmem_limit_bytes=limit * mega),
        cost_estimate=pl.CostEstimate(flops=flops, bytes_accessed=moved, transcendentals=0),
        name=name,
    )(*args)


def slots_body(experts, capacity, row_ref, col_ref, code_row, code_col):
    seq = row_ref.shape[1]
    half = capacity // 2
    quarter = (experts // 2) * half
    first = lax.broadcasted_iota(jnp.int32, (seq, seq), 0)
    second = lax.broadcasted_iota(jnp.int32, (seq, seq), 1)

    def code(route, slot):
        upper = jnp.where(slot >= half, 1, 0)
        return (2 * (route & 1) + upper) * quarter + (route >> 1) * half + slot - half * upper

    route = col_ref[...]
    chosen = route == lax.broadcasted_iota(jnp.int32, (seq, experts), 1)
    count = mm((second < first).astype(bf16), chosen.astype(bf16))
    slot = jnp.sum(jnp.where(chosen, count, 0.0), axis=1, keepdims=True).astype(jnp.int32)
    code_col[...] = code(route, slot)
    route = row_ref[...]
    chosen = route == lax.broadcasted_iota(jnp.int32, (experts, seq), 0)
    count = mm(chosen.astype(bf16), (first < second).astype(bf16))
    slot = jnp.sum(jnp.where(chosen, count, 0.0), axis=0, keepdims=True).astype(jnp.int32)
    code_row[...] = code(route, slot)


def span(i0, seq):
    start = max(0, i0 - reach)
    end = min(seq, i0 + rows_q + reach)
    return start, end, start - (i0 - reach)


def attend_body(
    t_ref, x0, x1, x2, x3, gain, weight, seg_row, seg_col, near, bias,
    x_all, normed, qkv, probs, ctx, tile,
):
    t = t_ref[0]
    own = x0.shape[0]
    seq = 4 * own
    heads = bias.shape[1]
    columns = heads * head_size
    for k, ref in enumerate((x0, x1, x2, x3)):
        at = pl.ds(pl.multiple_of((t ^ k) * own, own), own)
        x = ref[...]
        x_all[at, :] = x
        x = x.astype(f32)
        inv = lax.rsqrt(jnp.mean(x * x, axis=1, keepdims=True) + epsilon)
        normed[at, :] = (x * inv * gain[...]).astype(bf16)
    for c in range(3):
        full = mm(normed[...], weight[c])
        for h in range(heads):
            qkv[c * heads + h] = full[:, h * head_size : (h + 1) * head_size].astype(bf16)
    bucket = near[...]
    for h in range(heads):
        line = jnp.zeros(bucket.shape, f32)
        for b in range(bias.shape[0]):
            line = jnp.where(bucket == b, bias[b, h], line)
        wide = jnp.broadcast_to(line, (rows_q, table))
        tile[h] = pltpu.roll(wide, 0, 1, stride=1, stride_axis=0)[:, :window]
    for i0 in range(0, seq, rows_q):
        start, end, off = span(i0, seq)
        same = seg_col[i0 : i0 + rows_q, :] == seg_row[:, start:end]
        parts = []
        for h in range(heads):
            query = qkv[h, i0 : i0 + rows_q, :]
            score = mm_nt(query, qkv[heads + h, start:end, :])
            score = jnp.where(same, score + tile[h, :, off : off + end - start], negative)
            score = jnp.exp(score - jnp.max(score, axis=1, keepdims=True))
            inv = 1.0 / jnp.sum(score, axis=1, keepdims=True)
            prob = (score * inv).astype(bf16)
            probs[h, i0 : i0 + rows_q, 0 : end - start] = prob
            parts.append(mm(prob, qkv[2 * heads + h, start:end, :]).astype(bf16))
        ctx[i0 : i0 + rows_q, :] = jnp.concatenate(parts[:2], axis=1)
        lane = 0 if i0 < seq // 2 else head_size
        at = seq + i0 % (seq // 2)
        ctx[at : at + rows_q, lane : lane + head_size] = parts[2]


def third(ctx, r0, rows, seq):
    lane = 0 if r0 < seq // 2 else head_size
    at = seq + r0 % (seq // 2)
    return ctx[at : at + rows, lane : lane + head_size]


def mid_body(
    t_ref, x_all, c0, c1, c2, c3, w0, w1, w2, w3, gain, code_row,
    h_one, h_own, rows, normed,
):
    t = t_ref[0]
    seq = x_all.shape[0]
    own = seq // 4
    quarter = rows.shape[0]
    ctxs = (c0, c1, c2, c3)
    weights = (w0, w1, w2, w3)
    pair = 2 * head_size
    packed = [
        jnp.concatenate([weights[2 * i][0:pair, :], weights[2 * i + 1][0:pair, :]], axis=0)
        for i in range(2)
    ]
    last = jnp.concatenate([w[pair : pair + head_size, :] for w in weights], axis=0)
    for r0 in range(0, seq, own):
        at = slice(r0, r0 + own)
        total = x_all[at, :].astype(f32)
        for i in range(2):
            left = jnp.concatenate([ctxs[2 * i][at, :], ctxs[2 * i + 1][at, :]], axis=1)
            total = total + mm(left, packed[i])
        left = jnp.concatenate([third(c, r0, own, seq) for c in ctxs], axis=1)
        total = total + mm(left, last)
        h_one[at, :] = total
        inv = lax.rsqrt(jnp.mean(total * total, axis=1, keepdims=True) + epsilon)
        normed[at, :] = (total * inv * gain[...]).astype(bf16)
    h_own[...] = h_one[pl.ds(pl.multiple_of(t * own, own), own), :]
    place = lax.broadcasted_iota(jnp.int32, (quarter, seq), 0) + t * quarter
    rows[...] = mm((place == code_row[...]).astype(bf16), normed[...]).astype(bf16)


def spread_body(t_ref, g0, g1, g2, g3, code_row, g_all, rows):
    t = t_ref[0]
    own = g0.shape[0]
    quarter = rows.shape[0]
    for k, ref in enumerate((g0, g1, g2, g3)):
        g_all[pl.ds(pl.multiple_of((t ^ k) * own, own), own), :] = ref[...]
    place = lax.broadcasted_iota(jnp.int32, (quarter, g_all.shape[0]), 0) + t * quarter
    rows[...] = mm((place == code_row[...]).astype(bf16), g_all[...]).astype(bf16)


gelu_scale = 0.7978845608028654
gelu_cubic = 0.044715


def expert_body(
    e_ref, r0, r1, g0, g1, w_in, w_out, router,
    back0, back1, grad0, grad1, hidden_out, gated_out, pre_out, rows_out, router_out,
):
    rows = jnp.concatenate([r0[...], r1[...]], axis=0)
    cot = jnp.concatenate([g0[...], g1[...]], axis=0).astype(f32)
    half = r0.shape[0]
    experts = router.shape[1]
    logits = mm(rows, router[...])
    logits = jnp.exp(logits - jnp.max(logits, axis=1, keepdims=True))
    prob = logits / jnp.sum(logits, axis=1, keepdims=True)
    mine = lax.broadcasted_iota(jnp.int32, prob.shape, 1) == e_ref[1]
    gate = jnp.sum(jnp.where(mine, prob, 0.0), axis=1, keepdims=True)
    pre = mm(rows, w_in[0])
    inner = jnp.tanh(gelu_scale * (pre + gelu_cubic * pre * pre * pre))
    hidden = (0.5 * pre * (1.0 + inner)).astype(bf16)
    slope = 0.5 * (1.0 + inner) + 0.5 * pre * (1.0 - inner * inner) * gelu_scale * (
        1.0 + 3.0 * gelu_cubic * pre * pre
    )
    part = mm(hidden, w_out[0])
    back = (gate * part).astype(bf16)
    back0[...] = back[:half]
    back1[...] = back[half:]
    grad_gate = jnp.sum(cot * part, axis=1, keepdims=True)
    gated = (gate * cot).astype(bf16)
    grad_pre = (mm_nt(gated, w_out[0]) * slope).astype(bf16)
    grad_logits = (gate * grad_gate * (jnp.where(mine, 1.0, 0.0) - prob)).astype(bf16)
    grad = mm_nt(grad_pre, w_in[0]) + mm_nt(grad_logits, router[...])
    grad = grad.astype(bf16)
    grad0[...] = grad[:half]
    grad1[...] = grad[half:]
    hidden_out[...] = hidden
    gated_out[...] = gated
    pre_out[...] = grad_pre
    rows_out[...] = rows
    router_out[...] = mm_tn(grad_logits, rows)


def expert(e_index, e_global, r0, r1, g0, g1, w_in, w_out, router):
    scalars = jnp.stack([e_index, e_global])
    half, width = r0.shape
    hidden = w_in.shape[2]
    rows = 2 * half
    experts = router.shape[1]
    outs = [shape((half, width), bf16)] * 4 + [
        shape((rows, hidden), bf16),
        shape((rows, width), bf16),
        shape((rows, hidden), bf16),
        shape((rows, width), bf16),
        shape((experts, width), f32),
    ]

    def whole(dims):
        return pl.BlockSpec(dims, lambda i, s: (0,) * len(dims))

    spec = pltpu.PrefetchScalarGridSpec(
        num_scalar_prefetch=1,
        grid=(1,),
        in_specs=[whole(r0.shape)] * 4
        + [
            pl.BlockSpec((1,) + w_in.shape[1:], lambda i, s: (s[0], 0, 0)),
            pl.BlockSpec((1,) + w_out.shape[1:], lambda i, s: (s[0], 0, 0)),
            whole(router.shape),
        ],
        out_specs=[whole(o.shape) for o in outs],
    )
    return pl.pallas_call(
        expert_body,
        out_shape=outs,
        grid_spec=spec,
        compiler_params=pltpu.CompilerParams(vmem_limit_bytes=56 * mega),
        cost_estimate=pl.CostEstimate(
            flops=8 * rows * hidden * width, bytes_accessed=12 * mega, transcendentals=0
        ),
        name="expert",
    )(scalars, r0, r1, g0, g1, w_in, w_out, router)


def expert_grad_body(e_ref, hid0, gat0, pre0, row0, hid1, gat1, pre1, row1, d_in, d_out):
    near = pl.program_id(0) == 0

    @pl.when(near)
    def _():
        d_in[0] = mm_tn(row0[...], pre0[...])
        d_out[0] = mm_tn(hid0[...], gat0[...])

    @pl.when(jnp.logical_not(near))
    def _():
        d_in[0] = mm_tn(row1[...], pre1[...])
        d_out[0] = mm_tn(hid1[...], gat1[...])


def expert_grads(e_index, first, second):
    rows, hidden = first[0].shape
    width = first[3].shape[1]

    def whole(a):
        return pl.BlockSpec(a.shape, lambda i, s: (0, 0))

    def place(i, s):
        return (s[0] * (1 - i) + (1 - s[0]) * i, 0, 0)

    spec = pltpu.PrefetchScalarGridSpec(
        num_scalar_prefetch=1,
        grid=(2,),
        in_specs=[whole(a) for a in (*first, *second)],
        out_specs=[
            pl.BlockSpec((1, width, hidden), place),
            pl.BlockSpec((1, hidden, width), place),
        ],
    )
    return pl.pallas_call(
        expert_grad_body,
        out_shape=[shape((2, width, hidden), f32), shape((2, hidden, width), f32)],
        grid_spec=spec,
        compiler_params=pltpu.CompilerParams(vmem_limit_bytes=56 * mega),
        cost_estimate=pl.CostEstimate(
            flops=8 * rows * hidden * width, bytes_accessed=20 * mega, transcendentals=0
        ),
        name="expert_grads",
    )(e_index[None], *first, *second)


def back_body(
    t_ref, b0, b1, b2, b3, code_col, h_one, gain, g_all, weight, ctx, probs, qkv, normed, router,
    grad_h, h_own, gctx, grad_v, early,
):
    t = t_ref[0]
    seq, width = h_one.shape
    own = seq // 4
    quarter = b0.shape[0]
    heads = gctx.shape[0]
    columns = heads * head_size
    sum_gain = jnp.zeros((1, width), f32)
    for r0 in range(0, seq, own):
        at = slice(r0, r0 + own)
        total = jnp.zeros((own, width), f32)
        for k, ref in enumerate((b0, b1, b2, b3)):
            place = lax.broadcasted_iota(jnp.int32, (own, quarter), 1) + (t ^ k) * quarter
            total = total + mm((place == code_col[at, :]).astype(bf16), ref[...])
        h = h_one[at, :]
        inv = lax.rsqrt(jnp.mean(h * h, axis=1, keepdims=True) + epsilon)
        n2 = h * inv
        sum_gain = sum_gain + jnp.sum(total * n2, axis=0, keepdims=True)
        a = total * gain[...]
        mean = jnp.mean(a * n2, axis=1, keepdims=True)
        full = g_all[at, :].astype(f32) + inv * (a - n2 * mean)
        grad_h[at, :] = full.astype(bf16)

        @pl.when(t * own == r0)
        def _():
            h_own[...] = full

        wide = mm_nt(grad_h[at, :], weight[...])
        for j in range(heads):
            gctx[j, at, :] = wide[:, j * head_size : (j + 1) * head_size].astype(bf16)
    for h in range(heads):
        sums = [None] * (seq // rows_q)
        for i0 in range(0, seq, rows_q):
            start, end, _ = span(i0, seq)
            add = mm_tn(probs[h, i0 : i0 + rows_q, 0 : end - start], gctx[h, i0 : i0 + rows_q, :])
            for j in range(start, end, rows_q):
                piece = add[j - start : j - start + rows_q]
                n = j // rows_q
                sums[n] = piece if sums[n] is None else sums[n] + piece
        for n, piece in enumerate(sums):
            grad_v[n * rows_q : (n + 1) * rows_q, h * head_size : (h + 1) * head_size] = (
                piece.astype(bf16)
            )
    early[0:columns, :] = mm_tn(grad_v[...], normed[...]).astype(bf16)
    flat = jnp.concatenate(
        [
            ctx[0:seq, :],
            jnp.concatenate([third(ctx, r, own, seq) for r in range(0, seq, own)], axis=0),
        ],
        axis=1,
    )
    early[columns : 2 * columns, :] = mm_tn(flat, grad_h[...]).astype(bf16)
    early[2 * columns :, :] = jnp.zeros((early.shape[0] - 2 * columns, width), bf16)
    experts = router.shape[0]
    early[2 * columns : 2 * columns + experts, :] = router[...].astype(bf16)
    early[2 * columns + experts : 2 * columns + experts + 1, :] = sum_gain.astype(bf16)


def attend_back_body(
    probs, qkv, gctx, normed, near,
    grad_q, grad_k, late, grad_bias, spill,
):
    heads, seq, _ = gctx.shape
    columns = heads * head_size
    buckets = grad_bias.shape[0]
    places = lax.broadcasted_iota(jnp.int32, (buckets, 128), 1)
    found = jnp.zeros((buckets, 128), f32)
    for h in range(heads):
        cols = slice(h * head_size, (h + 1) * head_size)
        sums = [None] * (seq // rows_q)
        spill[...] = jnp.zeros(spill.shape, f32)
        for i0 in range(0, seq, rows_q):
            start, end, off = span(i0, seq)
            at = slice(i0, i0 + rows_q)
            prob = probs[h, at, 0 : end - start].astype(f32)
            grad = mm_nt(gctx[h, at, :], qkv[2 * heads + h, start:end, :])
            both = prob * grad
            delta = jnp.sum(both, axis=1, keepdims=True)
            score = both - prob * delta
            spill[:, off : off + end - start] += score
            score = score.astype(bf16)
            grad_q[at, cols] = mm(score, qkv[heads + h, start:end, :]).astype(bf16)
            add = mm_tn(score, qkv[h, at, :])
            for j in range(start, end, rows_q):
                piece = add[j - start : j - start + rows_q]
                n = j // rows_q
                sums[n] = piece if sums[n] is None else sums[n] + piece
        for n, piece in enumerate(sums):
            grad_k[n * rows_q : (n + 1) * rows_q, cols] = piece.astype(bf16)
        strip = jnp.zeros((8, table), f32)
        for a in range(0, rows_q, 8):
            strip = strip + pltpu.roll(spill[a : a + 8, :], (table - a) % table, 1)
        line = lax.broadcasted_iota(jnp.int32, strip.shape, 0)
        for bit in (1, 2, 4):
            strip = jnp.where((line & bit) != 0, pltpu.roll(strip, table - bit, 1), strip)
        strip = jnp.sum(strip, axis=0, keepdims=True)
        chosen = near[...] == lax.broadcasted_iota(jnp.int32, (buckets, table), 0)
        per = jnp.sum(jnp.where(chosen, strip, 0.0), axis=1, keepdims=True)
        found = found + jnp.where(places == h, per, 0.0)
    grad_bias[...] = found
    late[0:columns, :] = mm_tn(grad_q[...], normed[...]).astype(bf16)
    late[columns : 2 * columns, :] = mm_tn(grad_k[...], normed[...]).astype(bf16)


def input_grad_body(t_ref, grad_q, grad_k, grad_v, weight, normed, gain, keep, send, sums):
    t = t_ref[0]
    seq, width = normed.shape
    own = seq // 4
    total_gain = jnp.zeros((1, width), f32)
    for k in range(4):
        at = pl.ds(pl.multiple_of((t ^ k) * own, own), own)
        part = mm_nt(grad_q[at, :], weight[0])
        part = part + mm_nt(grad_k[at, :], weight[1])
        part = part + mm_nt(grad_v[at, :], weight[2])
        total_gain = total_gain + jnp.sum(part * normed[at, :].astype(f32), axis=0, keepdims=True)
        out = keep if k in (0, 2) else send
        out[(k // 2) * own : (k // 2 + 1) * own, :] = part.astype(bf16)
    sums[...] = total_gain / gain[...]


def last_body(kept, got, far, x_ref, gain, h_own, grad):
    total = kept[...].astype(f32) + got[...].astype(f32) + far[...].astype(f32)
    x = x_ref[...].astype(f32)
    inv = lax.rsqrt(jnp.mean(x * x, axis=1, keepdims=True) + epsilon)
    n1 = x * inv
    a = total * gain[...]
    grad[...] = h_own[...] + inv * (a - n1 * jnp.mean(a * n1, axis=1, keepdims=True))


def output_body(t_ref, f0, f1, f2, f3, code_col, h_own, out):
    t = t_ref[0]
    own = h_own.shape[0]
    quarter = f0.shape[0]
    total = h_own[...]
    codes = code_col[pl.ds(pl.multiple_of(t * own, own), own), :]
    for k, ref in enumerate((f0, f1, f2, f3)):
        place = lax.broadcasted_iota(jnp.int32, (own, quarter), 1) + (t ^ k) * quarter
        total = total + mm((place == codes).astype(bf16), ref[...])
    out[...] = total.astype(bf16)


def turn(value):
    return lax.all_to_all(value, "dp", split_axis=0, concat_axis=0, tiled=True)


def reduce_dp(part):
    n = lax.axis_size("dp")
    got = turn(part).reshape(n, part.shape[0] // n, part.shape[1])
    return jnp.sum(got.astype(f32), axis=0).astype(bf16)


def gather_dp(share):
    n = lax.axis_size("dp")
    wide = jnp.broadcast_to(share[None], (n,) + share.shape)
    return turn(wide.reshape(n * share.shape[0], share.shape[1])).reshape((n,) + share.shape)


def per_device(
    inputs,
    segments,
    buckets,
    routes,
    qkv_weight,
    out_weight,
    rel_bias,
    norm_attn,
    norm_moe,
    router_weight,
    expert_in,
    expert_out,
    cotangent,
):
    own, width = inputs.shape
    seq = 4 * own
    dp = lax.axis_size("dp")
    experts = router_weight.shape[1]
    capacity = max(2, 5 * seq // (4 * experts))
    quarter = (experts // 2) * (capacity // 2)
    columns = qkv_weight.shape[2]
    heads = rel_bias.shape[1]
    t = lax.axis_index("tensor").astype(jnp.int32)
    t_one = t[None]
    x_side = t // 2
    first_expert = 2 * lax.axis_index("dp").astype(jnp.int32)
    gain_attn = norm_attn[None, :]
    gain_moe = norm_moe[None, :]
    near = lax.slice_in_dim(buckets, seq - 1 - reach, seq - 1 - reach + table, axis=0)[None, :]
    seg_col = segments.reshape(seq, 1)
    route_row = routes.reshape(1, seq)
    route_col = routes.reshape(seq, 1)

    xs = gather4(inputs)
    gs = gather4(cotangent)
    ws = gather4(out_weight)
    code_row, code_col = run(
        functools.partial(slots_body, experts, capacity),
        [shape((1, seq), jnp.int32), shape((seq, 1), jnp.int32)],
        [route_row, route_col],
        name="slots",
    )
    x_all, normed, qkv, probs, ctx = run(
        attend_body,
        [
            shape((seq, width), bf16),
            shape((seq, width), bf16),
            shape((3 * heads, seq, head_size), bf16),
            shape((heads, seq, window), bf16),
            shape((seq + seq // 2, 2 * head_size), bf16),
        ],
        [t_one, *xs, gain_attn, qkv_weight, segments, seg_col, near, rel_bias],
        smem=(0, 10),
        scratch=[pltpu.VMEM((heads, rows_q, window), f32)],
        flops=4 * 1024 * mega,
        name="attend",
    )
    g_all, g_rows = run(
        spread_body,
        [shape((seq, width), bf16), shape((quarter, width), bf16)],
        [t_one, *gs, code_row],
        smem=(0,),
        flops=512 * mega,
        name="spread",
    )
    g_rows = turn(g_rows)
    gr = gather4(g_rows)
    cs = gather4(ctx)
    h_one, h_own, rows = run(
        mid_body,
        [
            shape((seq, width), f32),
            shape((own, width), f32),
            shape((quarter, width), bf16),
        ],
        [t_one, x_all, *cs, *ws, gain_moe, code_row],
        smem=(0,),
        scratch=[pltpu.VMEM((seq, width), bf16)],
        flops=2 * 1024 * mega,
        name="mid",
    )
    rows = turn(rows)
    rs = gather4(rows)
    near_out = expert(
        x_side, first_expert + x_side, rs[0], rs[1], gr[0], gr[1], expert_in, expert_out, router_weight
    )
    far_out = expert(
        1 - x_side, first_expert + 1 - x_side, rs[2], rs[3], gr[2], gr[3],
        expert_in, expert_out, router_weight,
    )
    grad_expert_in, grad_expert_out = expert_grads(x_side, near_out[4:8], far_out[4:8])

    def back_home(near_mine, near_peer, far_mine, far_peer):
        far = far_mine + core_hop(far_peer)
        kept = near_mine + core_hop(near_peer)
        return turn(kept + x_hop(far))

    home = back_home(near_out[2], near_out[3], far_out[2], far_out[3])
    bs = gather4(home)
    fwd = back_home(near_out[0], near_out[1], far_out[0], far_out[1])
    fs = gather4(fwd)
    router_part = near_out[8] + far_out[8]
    router_part = router_part + core_hop(router_part)
    router_part = router_part + x_hop(router_part)
    small = -(-(experts + 1) // 64) * 64
    grad_h, gh_own, gctx, grad_v, early = run(
        back_body,
        [
            shape((seq, width), bf16),
            shape((own, width), f32),
            shape((heads, seq, head_size), bf16),
            shape((seq, columns), bf16),
            shape((2 * columns + small, width), bf16),
        ],
        [t_one, *bs, code_col, h_one, gain_moe, g_all, out_weight, ctx, probs, qkv, normed, router_part],
        smem=(0,),
        limit=56,
        flops=5 * 1024 * mega,
        name="back",
    )
    early_share = reduce_dp(early)
    grad_q, grad_k, late, grad_bias = run(
        attend_back_body,
        [
            shape((seq, columns), bf16),
            shape((seq, columns), bf16),
            shape((2 * columns, width), bf16),
            shape((rel_bias.shape[0], 128), f32),
        ],
        [probs, qkv, gctx, normed, near],
        scratch=[pltpu.VMEM((rows_q, table), f32)],
        limit=56,
        flops=4 * 1024 * mega,
        name="attend_back",
    )
    late_share = reduce_dp(late)
    keep, send, gain_part = run(
        input_grad_body,
        [
            shape((2 * own, width), bf16),
            shape((2 * own, width), bf16),
            shape((1, width), f32),
        ],
        [t_one, grad_q, grad_k, grad_v, qkv_weight, normed, gain_attn],
        smem=(0,),
        flops=1024 * mega,
        name="input_grad",
    )
    got = core_hop(send)
    far = x_hop(keep[own:] + got[own:])
    (grad_inputs,) = run(
        last_body,
        [shape((own, width), f32)],
        [keep[:own], got[:own], far, inputs, gain_attn, gh_own],
        name="last",
    )
    gain_part = gain_part + core_hop(gain_part)
    gain_part = gain_part + x_hop(gain_part)
    (output,) = run(
        output_body,
        [shape((own, width), bf16)],
        [t_one, *fs, code_col, h_own],
        smem=(0,),
        name="output",
    )
    bias_line = jnp.pad(
        grad_bias[:, :heads].reshape(1, -1), ((0, 0), (0, width - heads * rel_bias.shape[0]))
    )
    extra = jnp.pad(jnp.concatenate([gain_part, bias_line], axis=0), ((0, 14), (0, 0))).astype(bf16)
    early_all = gather_dp(early_share).reshape(early.shape)
    late_rows = late_share.shape[0]
    late_all = gather_dp(jnp.concatenate([late_share, extra], axis=0))
    extra = jnp.sum(late_all[:, late_rows : late_rows + 2].astype(f32), axis=0)
    late_all = late_all[:, :late_rows].reshape(late.shape)
    grad_qkv_weight = jnp.stack(
        [late_all[:columns].T, late_all[columns:].T, early_all[:columns].T]
    ).astype(f32)
    grad_out_weight = early_all[columns : 2 * columns].astype(f32)
    grad_router = early_all[2 * columns : 2 * columns + experts].T.astype(f32)
    grad_norm_moe = early_all[2 * columns + experts].astype(f32)
    grad_rel_bias = extra[1, : heads * rel_bias.shape[0]].reshape(rel_bias.shape)
    return (
        output,
        grad_inputs,
        grad_qkv_weight,
        grad_out_weight,
        grad_rel_bias,
        extra[0],
        grad_norm_moe,
        grad_router,
        grad_expert_in,
        grad_expert_out,
    )


def solution(mesh):
    placed = (
        P(("dp", "tensor"), None),
        P("dp", None),
        P(),
        P("dp", None, None),
        P(None, None, "tensor"),
        P("tensor", None),
        P(None, "tensor"),
        P(),
        P(),
        P(),
        P("dp", None, "tensor"),
        P("dp", "tensor", None),
        P(("dp", "tensor"), None),
    )
    return jax.shard_map(
        per_device,
        mesh=mesh,
        in_specs=placed,
        out_specs=(
            P(("dp", "tensor"), None),
            P(("dp", "tensor"), None),
            P(None, None, "tensor"),
            P("tensor", None),
            P(None, "tensor"),
            P(),
            P(),
            P(),
            P("dp", None, "tensor"),
            P("dp", "tensor", None),
        ),
        check_vma=False,
    )
```

time: 824 us -> 329 us (0.40)
  local copies, waits for them, and re-layouts: 266 us -> 21.8 us
  blocking collectives: 264 us -> 20.1 us
  Pallas kernels: 0 us -> 94.8 us
  matrix products: 81.1 us -> 0 us
  starting transfers between devices: 0.58 us -> 65.6 us
  other arithmetic: 63.8 us -> 15.4 us
  waiting for transfers between devices: 121 us -> 104 us
  between operations: 15.4 us -> 1.28 us
    all_to_all x4 -> x1, blocking collectives: 200 us -> 20.1 us  [turn(): return lax.all_to_all(value, 'dp', split_axis=0, concat_axis=0, tiled=True)]
    unnamed x180 -> x92, local copies, waits for them, and re-layouts: 120 us -> 16.2 us
    pallas_call x0 -> x12, Pallas kernels: none -> 94.8 us  [the longest x9 68.3 us: run(): pl.pallas_call(body, out_shape=outs, in_specs=specs, out_specs=[pl.BlockS...]
    reduce_scatter x4 -> x0, waiting for transfers between devices: 88.9 us -> none  [the longest x2 50.6 us: to_tokens(): lax.psum_scatter(rows_of(dispatch, returned).astype(jnp.bfloat16), 'tenso...]
    dot_general x32 -> x0, matrix products: 78.3 us -> none  [the longest x2 7.66 us: add_rows(): return jnp.dot(dispatch, incoming, preferred_element_type=jnp.float32)]
    reshape x6 -> x3, local copies, waits for them, and re-layouts: 67.6 us -> 1.23 us  [the longest x1 0.9 us: per_device(): seg_col = segments.reshape(seq, 1)]
    psum x2 -> x0, blocking collectives: 63.8 us -> none  [the longest x1 44.2 us: per_device(): lax.psum((grad_norm_attn, grad_norm_moe, grad_router), ('dp', 'tensor'))]
    ppermute x0 -> x36, waiting for transfers between devices: none -> 63.3 us  [the longest x13 58.8 us: x_hop(): return lax.ppermute(value, 'tensor', x_pairs)]
  transfers between devices with their start and end apart: 9 -> 43, of which waited for: 6 -> 17; matrix products, arithmetic and copies ran while one was open for 39% -> 4% of each run, Pallas kernels for 0% -> 29%
where the time goes in v1:
time: 329 us; the launch traced here: 323 us
  waiting for transfers between devices  104 us (32%)
  Pallas kernels  94.8 us (29%)
  starting transfers between devices  65.6 us (20%)
  local copies, waits for them, and re-layouts  21.8 us (7%)
  blocking collectives  20.1 us (6%)
  other arithmetic  15.4 us (5%)
    pallas_call x9, Pallas kernels, run(): pl.pallas_call(body, out_shape=outs, in_specs=specs, out_specs=[pl.BlockS...  68.3 us
    ppermute x13, waiting for transfers between devices, x_hop(): return lax.ppermute(value, 'tensor', x_pairs)  58.8 us
    all_to_all x7, starting transfers between devices, turn(): return lax.all_to_all(value, 'dp', split_axis=0, concat_axis=0, tiled=True)  45.2 us
    all_to_all x7, waiting for transfers between devices, turn(): return lax.all_to_all(value, 'dp', split_axis=0, concat_axis=0, tiled=True)  41.1 us
    all_to_all x1, blocking collectives, turn(): return lax.all_to_all(value, 'dp', split_axis=0, concat_axis=0, tiled=True)  20.1 us
    ppermute x13, starting transfers between devices, x_hop(): return lax.ppermute(value, 'tensor', x_pairs)  16.9 us
    pallas_call x2, Pallas kernels, expert(): pl.pallas_call(expert_body, out_shape=outs, grid_spec=spec, compiler_para...  16.9 us
    unnamed x92, local copies, waits for them, and re-layouts  16.2 us
  transfers between devices with their start and end apart: 43, of which 17 were waited for; matrix products, arithmetic and copies ran while one was open for 4% of the time, Pallas kernels for 29%

profile of v1, /device:TPU:10, one launch (start us, length us, event | category | flops | bytes accessed | tf_op | source)
XLA Modules:
  0.0 323.3 jit_solution(6195967580463819614)
XLA Ops:
  1.3 1.5 collective-permute-start.11
  2.8 10.2 %collective-permute-done.1.x2 = bf16[256,768]{1,0:T(8,128)(2,1)S(1)} collective-permute-done((bf16[256,768]{1,0:T(8,128)(2,1)}, bf16[256,768]{1,0:T(8,128)(2,1)S(1)}, u32[]{:S(2)}, u32[]{:S(2)}) %collective-permute-start.1) | collective-permute-done | bytes 393248 | tf_op jit(solution)/shard_map/ppermute | solution.py:30
  14.2 1.5 copy.29.weight
  16.8 3.6 %collective-permute-done.11.g2 = bf16[256,768]{1,0:T(8,128)(2,1)} collective-permute-done((bf16[256,768]{1,0:T(8,128)(2,1)}, bf16[256,768]{1,0:T(8,128)(2,1)}, u32[]{:S(2)}, u32[]{:S(2)}) %collective-permute-start.11) | collective-permute-done | bytes 393248 | tf_op jit(solution)/shard_map/ppermute | solution.py:30
  21.1 1.0 copy-done.22
  22.1 1.0 copy-done.24
  23.1 14.7 %attend.1 = (bf16[1024,768]{1,0:T(8,128)(2,1)S(1)}, bf16[1024,768]{1,0:T(8,128)(2,1)}, bf16[9,1024,64]{2,1,0:T(8,128)(2,1)}, bf16[3,1024,640]{2,1,0:T(8,128)(2,1)}, bf16[1536,128]{1,0:T(8,128)(2,1)S(1)}) custom-call(s32[1]{0:T(128)} %bitcast.t_ref, bf16[256,768]{1,0:T(8,128)(2,1)S(1)} %copy-done.11, bf16[256,768]{1,0:T(8,128)(2,1)S(1)} %copy-done.24, ...), custom_call_target="tpu_custom_call" | custom-call | flops 4294967296 | bytes 11123076 | tf_op jit(solution)/shard_map/attend/pallas_call | solution.py:66
  37.8 1.1 copy-done.27
  39.7 1.1 slots.1
  41.6 2.8 spread.1
  44.4 1.1 copy-done.26
  45.6 6.6 %all-to-all-start.1 = ((bf16[8,40,768]{2,1,0:T(8,128)(2,1)}), bf16[8,40,768]{2,1,0:T(8,128)(2,1)S(1)}, u32[]{:S(2)}, u32[]{:S(2)}) async-start(bf16[8,40,768]{2,1,0:T(8,128)(2,1)} %bitcast.8), calls=%async_computation.1 | async-start | bytes 983040 | tf_op jit(solution)/shard_map/all_to_all | solution.py:473
  52.2 1.6 collective-permute-start.7
  54.2 6.6 %collective-permute-done.7.w2 = bf16[192,768]{1,0:T(8,128)(2,1)S(1)} collective-permute-done((bf16[192,768]{1,0:T(8,128)(2,1)S(1)}, bf16[192,768]{1,0:T(8,128)(2,1)S(1)}, u32[]{:S(2)}, u32[]{:S(2)}) %collective-permute-start.7) | collective-permute-done | bytes 294944 | tf_op jit(solution)/shard_map/ppermute | solution.py:30
  60.8 1.5 collective-permute-done.8.w3
  62.4 1.4 copy-done.28
  63.8 3.9 %mid.1 = (f32[1024,768]{1,0:T(8,128)}, f32[256,768]{1,0:T(8,128)S(1)}, bf16[320,768]{1,0:T(8,128)(2,1)}) custom-call(s32[1]{0:T(128)} %bitcast.t_ref, bf16[1024,768]{1,0:T(8,128)(2,1)S(1)} %copy-done.28, bf16[1536,128]{1,0:T(8,128)(2,1)S(1)} %get-tuple-element.54.c0.ctx, bf16[1536,128]{1,0:T(8,128)(2,1)S(1)} %collective-permute-done.3.c1, ...), custom_call_target="tpu_custom_call" | custom-call | flops 2147483648 | bytes 8756228 | tf_op jit(solution)/shard_map/mid/pallas_call | solution.py:66
  68.6 6.0 %all-to-all-start = ((bf16[8,40,768]{2,1,0:T(8,128)(2,1)}), bf16[8,40,768]{2,1,0:T(8,128)(2,1)S(1)}, u32[]{:S(2)}, u32[]{:S(2)}) async-start(bf16[8,40,768]{2,1,0:T(8,128)(2,1)} %bitcast.6), calls=%async_computation | async-start | bytes 983040 | tf_op jit(solution)/shard_map/all_to_all | solution.py:473
  74.6 1.5 collective-permute-start.17
  76.1 11.4 %all-to-all-done = bf16[8,40,768]{2,1,0:T(8,128)(2,1)S(1)} async-done(((bf16[8,40,768]{2,1,0:T(8,128)(2,1)}), bf16[8,40,768]{2,1,0:T(8,128)(2,1)S(1)}, u32[]{:S(2)}, u32[]{:S(2)}) %all-to-all-start) | async-done | bytes 491552 | tf_op jit(solution)/shard_map/all_to_all | solution.py:473
  87.5 1.5 collective-permute-start.15
  89.0 8.9 %collective-permute-done.15.r0 = bf16[320,768]{1,0:T(8,128)(2,1)S(1)} collective-permute-done((bf16[320,768]{1,0:T(8,128)(2,1)S(1)}, bf16[320,768]{1,0:T(8,128)(2,1)S(1)}, u32[]{:S(2)}, u32[]{:S(2)}) %collective-permute-start.15) | collective-permute-done | bytes 491552 | tf_op jit(solution)/shard_map/ppermute | solution.py:30
  99.9 8.3 %expert.3 = (bf16[320,768]{1,0:T(8,128)(2,1)}, bf16[320,768]{1,0:T(8,128)(2,1)}, bf16[320,768]{1,0:T(8,128)(2,1)}, bf16[320,768]{1,0:T(8,128)(2,1)}, bf16[640,76...) custom-call(s32[2]{0:T(128)} %pad_add_fusion.1.e_ref, ...), custom_call_target="tpu_custom_call" | custom-call | flops 3019898880 | bytes 12582912 | tf_op jit(solution)/shard_map/expert/pallas_call | solution.py:271
  109.4 8.5 %expert.2 = (bf16[320,768]{1,0:T(8,128)(2,1)}, bf16[320,768]{1,0:T(8,128)(2,1)}, bf16[320,768]{1,0:T(8,128)(2,1)}, bf16[320,768]{1,0:T(8,128)(2,1)}, bf16[640,76...) custom-call(s32[2]{0:T(128)} %pad_add_fusion.e_ref, ...), custom_call_target="tpu_custom_call" | custom-call | flops 3019898880 | bytes 12582912 | tf_op jit(solution)/shard_map/expert/pallas_call | solution.py:271
  118.2 1.6 collective-permute-start.26
  120.1 11.8 %collective-permute-done.26 = bf16[320,768]{1,0:T(8,128)(2,1)S(1)} collective-permute-done((bf16[320,768]{1,0:T(8,128)(2,1)S(1)}, bf16[320,768]{1,0:T(8,128)(2,1)S(1)}, u32[]{:S(2)}, u32[]{:S(2)}) %collective-permute-start.26) | collective-permute-done | bytes 491552 | tf_op jit(solution)/shard_map/ppermute | solution.py:30
  131.9 2.0 add_add_fusion
  133.9 7.6 %all-to-all-start.3 = ((bf16[8,40,768]{2,1,0:T(8,128)(2,1)}), bf16[8,40,768]{2,1,0:T(8,128)(2,1)S(1)}, u32[]{:S(2)}, u32[]{:S(2)}) async-start(bf16[8,40,768]{2,1,0:T(8,128)(2,1)} %bitcast.14), calls=%async_computation.3 | async-start | bytes 983040 | tf_op jit(solution)/shard_map/all_to_all | solution.py:473
  141.4 12.4 %all-to-all-done.3 = bf16[8,40,768]{2,1,0:T(8,128)(2,1)S(1)} async-done(((bf16[8,40,768]{2,1,0:T(8,128)(2,1)}), bf16[8,40,768]{2,1,0:T(8,128)(2,1)S(1)}, u32[]{:S(2)}, u32[]{:S(2)}) %all-to-all-start.3) | async-done | bytes 491552 | tf_op jit(solution)/shard_map/all_to_all | solution.py:473
  153.8 1.5 collective-permute-start.28
  156.3 11.8 %collective-permute-done.28.b2 = bf16[320,768]{1,0:T(8,128)(2,1)} collective-permute-done((bf16[320,768]{1,0:T(8,128)(2,1)S(1)}, bf16[320,768]{1,0:T(8,128)(2,1)}, u32[]{:S(2)}, u32[]{:S(2)}) %collective-permute-start.28) | collective-permute-done | bytes 491552 | tf_op jit(solution)/shard_map/ppermute | solution.py:30
  168.7 1.3 collective-permute-done.30
  170.0 1.5 collective-permute-start.31
  171.6 3.9 %collective-permute-done.31 = f32[16,768]{1,0:T(8,128)S(1)} collective-permute-done((f32[16,768]{1,0:T(8,128)S(1)}, f32[16,768]{1,0:T(8,128)S(1)}, u32[]{:S(2)}, u32[]{:S(2)}) %collective-permute-start.31) | collective-permute-done | bytes 49184 | tf_op jit(solution)/shard_map/ppermute | solution.py:30
  177.0 7.7 %all-to-all-start.2 = ((bf16[8,40,768]{2,1,0:T(8,128)(2,1)}), bf16[8,40,768]{2,1,0:T(8,128)(2,1)S(1)}, u32[]{:S(2)}, u32[]{:S(2)}) async-start(bf16[8,40,768]{2,1,0:T(8,128)(2,1)} %bitcast.12), calls=%async_computation.2 | async-start | bytes 983040 | tf_op jit(solution)/shard_map/all_to_all | solution.py:473
  184.8 27.8 %back.1 = (bf16[1024,768]{1,0:T(8,128)(2,1)}, f32[256,768]{1,0:T(8,128)}, bf16[3,1024,64]{2,1,0:T(8,128)(2,1)}, bf16[1024,192]{1,0:T(8,128)(2,1)}, bf16[448,768]{1,0:T(8,128)(2,1)}) custom-call(s32[1]{0:T(128)} %bitcast.t_ref, bf16[320,768]{1,0:T(8,128)(2,1)} %bitcast.53, bf16[320,768]{1,0:T(8,128)(2,1)} %collective-permute-done.27.b1, ...), custom_call_target="tpu_custom_call" | custom-call | flops 5368709120 | bytes 17947652 | tf_op jit(solution)/shard_map/back/pallas_call | solution.py:66
  212.6 13.4 %attend_back.1 = (bf16[1024,192]{1,0:T(8,128)(2,1)}, bf16[1024,192]{1,0:T(8,128)(2,1)}, bf16[384,768]{1,0:T(8,128)(2,1)}, f32[32,128]{1,0:T(8,128)}) custom-call(bf16[3,1024,640]{2,1,0:T(8,128)(2,1)} %get-tuple-element.64.probs, bf16[9,1024,64]{2,1,0:T(8,128)(2,1)} %get-tuple-element.65.qkv, bf16[3,1024,64]{2,1,0:T(8,128)(2,1)} %get-tuple-element.75.gctx, ...), custom_call_target="tpu_custom_call" | custom-call | flops 4294967296 | bytes 8473600 | tf_op jit(solution)/shard_map/attend_back/pallas_call | solution.py:66
  226.0 20.1 %all_to_all.77 = bf16[8,48,768]{2,1,0:T(8,128)(2,1)} all-to-all(bf16[8,48,768]{2,1,0:T(8,128)(2,1)} %bitcast.44), channel_id=1, replica_groups=mesh['dp'=8,'tensor'=4] {'dp'}, dimensions={0} | all-to-all | bytes 1179648 | tf_op jit(solution)/shard_map/all_to_all | solution.py:473
  246.0 5.5 %all-to-all-start.6 = ((bf16[8,56,768]{2,1,0:T(8,128)(2,1)}), bf16[8,56,768]{2,1,0:T(8,128)(2,1)}, u32[]{:S(2)}, u32[]{:S(2)}) async-start(bf16[8,56,768]{2,1,0:T(8,128)(2,1)} %bitcast.43), calls=%async_computation.6 | async-start | bytes 1376256 | tf_op jit(solution)/shard_map/all_to_all | solution.py:473
  251.5 1.0 copy-done.6
  252.6 1.0 copy-done.7
  253.6 1.0 copy-done.8
  254.7 1.5 input_grad.1
  257.9 1.2 collective-permute-done.34
  259.1 1.5 collective-permute-start.35
  260.7 2.0 collective-permute-done.35
  262.7 1.1 reduce_sum.33
  263.9 2.8 all-to-all-done.6
  266.6 0.9 broadcast_in_dim.29
  267.6 5.7 %all-to-all-start.5 = ((bf16[8,64,768]{2,1,0:T(8,128)(2,1)}), bf16[8,64,768]{2,1,0:T(8,128)(2,1)}, u32[]{:S(2)}, u32[]{:S(2)}) async-start(bf16[8,64,768]{2,1,0:T(8,128)(2,1)} %broadcast_in_dim.29), calls=%async_computation.5 | async-start | bytes 1572864 | tf_op jit(solution)/shard_map/all_to_all | solution.py:473
  273.3 1.5 collective-permute-start.22
  274.8 1.2 reduce_sum.34
  276.0 14.5 %all-to-all-done.5 = bf16[8,64,768]{2,1,0:T(8,128)(2,1)} async-done(((bf16[8,64,768]{2,1,0:T(8,128)(2,1)}), bf16[8,64,768]{2,1,0:T(8,128)(2,1)}, u32[]{:S(2)}, u32[]{:S(2)}) %all-to-all-start.5) | async-done | bytes 786464 | tf_op jit(solution)/shard_map/all_to_all | solution.py:473
  291.4 6.1 %all-to-all-start.7 = ((bf16[8,56,768]{2,1,0:T(8,128)(2,1)}), bf16[8,56,768]{2,1,0:T(8,128)(2,1)}, u32[]{:S(2)}, u32[]{:S(2)}) async-start(bf16[8,56,768]{2,1,0:T(8,128)(2,1)} %broadcast_in_dim.30), calls=%async_computation.7 | async-start | bytes 1376256 | tf_op jit(solution)/shard_map/all_to_all | solution.py:473
  298.1 1.2 slice_add_fusion
  299.4 1.5 collective-permute-start.33
  300.9 9.6 %expert_grads.1 = (f32[2,768,768]{2,1,0:T(8,128)}, f32[2,768,768]{2,1,0:T(8,128)}) custom-call(s32[1]{0:T(128)} %bitcast.1.e_ref, bf16[640,768]{1,0:T(8,128)(2,1)} %get-tuple-element.86.hid0, bf16[640,768]{1,0:T(8,128)(2,1)} %get-tuple-element.87.gat0, bf16[640,768]{1,0:T(8,128)(2,1)} %get-tuple-element.88.pre0, bf16[640,768]{1,0:T(8,128)(2,1)} %get-tuple-element.89.row0, ...), custom_call_target="tpu_custom_call" | custom-call | flops 3019898880 | bytes 20971520 | tf_op jit(solution)/shard_map/expert_grads/pallas_call | solution.py:316
  310.6 1.8 output.1
  312.4 1.4 last.1
  315.3 1.9 slice_convert_fusion
  317.2 1.3 fusion.3
  318.5 1.4 convert_bitcast_fusion
  320.6 1.1 fusion.4
  321.7 1.3 maximum_convert_fusion
  (162 shorter events, 19.1 us)
Async XLA Ops:
  0.6 20.5 %copy-start.11 = (bf16[256,768]{1,0:T(8,128)(2,1)S(1)}, bf16[256,768]{1,0:T(8,128)(2,1)}, u32[]{:S(2)}) copy-start(bf16[256,768]{1,0:T(8,128)(2,1)} %x_ref.1) | copy-start | bytes 1179652
  0.7 20.5 %copy-start.14 = (s32[1,1024]{1,0:T(1,128)S(1)}, s32[1,1024]{1,0:T(1,128)}, u32[]{:S(2)}) copy-start(s32[1,1024]{1,0:T(1,128)} %seg_row.1) | copy-start | bytes 12292
  0.7 15.9 %copy-start.41 = (s32[2047]{0:T(1024)S(1)}, s32[2047]{0:T(1024)}, u32[]{:S(2)}) copy-start(s32[2047]{0:T(1024)} %param.15) | copy-start | bytes 24568
  0.7 16.0 %copy-start.40 = (f32[32,3]{0,1:T(4,128)S(1)}, f32[32,3]{0,1:T(4,128)}, u32[]{:S(2)}) copy-start(f32[32,3]{0,1:T(4,128)} %param.19) | copy-start | bytes 1156
  0.7 12.3 %collective-permute-start.1 = (bf16[256,768]{1,0:T(8,128)(2,1)}, bf16[256,768]{1,0:T(8,128)(2,1)S(1)}, u32[]{:S(2)}, u32[]{:S(2)}) collective-permute-start(bf16[256,768]{1,0:T(8,128)(2,1)} %x_ref.1), channel_id=1, source_target_pairs={{0,2},{2,0},{1,3},{3,1},{4,6},{6,4},{5,7},{7,5},{8,10},{10,8},{9,1... | collective-permute-start | bytes 1179656 | tf_op jit(solution)/shard_map/ppermute | solution.py:30
  1.3 19.1 %collective-permute-start.11 = (bf16[256,768]{1,0:T(8,128)(2,1)}, bf16[256,768]{1,0:T(8,128)(2,1)}, u32[]{:S(2)}, u32[]{:S(2)}) collective-permute-start(bf16[256,768]{1,0:T(8,128)(2,1)} %g0.1), channel_id=1, source_target_pairs={{0,2},{2,0},{1,3},{3,1},{4,6},{6,4},{5,7},{7,5},{8,10},{10,8},{9,1... | collective-permute-start | bytes 1179656 | tf_op jit(solution)/shard_map/ppermute | solution.py:30
  2.8 17.6 %collective-permute-start = (bf16[256,768]{1,0:T(8,128)(2,1)}, bf16[256,768]{1,0:T(8,128)(2,1)S(1)}, u32[]{:S(2)}, u32[]{:S(2)}) collective-permute-start(bf16[256,768]{1,0:T(8,128)(2,1)} %x_ref.1), channel_id=1, source_target_pairs={{0,1},{1,0},{2,3},{3,2},{4,5},{5,4},{6,7},{7,6},{8,9},{9,8},{10,11... | collective-permute-start | bytes 1179656 | tf_op jit(solution)/shard_map/ppermute | solution.py:26
  13.0 8.1 %collective-permute-start.2 = (bf16[256,768]{1,0:T(8,128)(2,1)S(1)}, bf16[256,768]{1,0:T(8,128)(2,1)}, u32[]{:S(2)}, u32[]{:S(2)}) collective-permute-start(bf16[256,768]{1,0:T(8,128)(2,1)S(1)} %collective-permute-done.1.x2), channel_id=1, source_target_pairs={{0,1},{1,0},{2,3},{3,2},{4,5},{5,4},{6,7},{7,6},{8,9},{9,8},{10,11... | collective-permute-start | bytes 1179656 | tf_op jit(solution)/shard_map/ppermute | solution.py:26
  13.0 28.6 %collective-permute-start.10 = (bf16[256,768]{1,0:T(8,128)(2,1)}, bf16[256,768]{1,0:T(8,128)(2,1)}, u32[]{:S(2)}, u32[]{:S(2)}) collective-permute-start(bf16[256,768]{1,0:T(8,128)(2,1)} %g0.1), channel_id=1, source_target_pairs={{0,1},{1,0},{2,3},{3,2},{4,5},{5,4},{6,7},{7,6},{8,9},{9,8},{10,11... | collective-permute-start | bytes 1179656 | tf_op jit(solution)/shard_map/ppermute | solution.py:26
  16.7 21.1 %copy-start.15 = (s32[1,768]{1,0:T(1,128)}, s32[1,768]{1,0:T(1,128)S(1)}, u32[]{:S(2)}) copy-start(s32[1,768]{1,0:T(1,128)S(1)} %broadcast_in_dim.27.near) | copy-start | bytes 9220
  20.3 21.3 %collective-permute-start.12 = (bf16[256,768]{1,0:T(8,128)(2,1)}, bf16[256,768]{1,0:T(8,128)(2,1)}, u32[]{:S(2)}, u32[]{:S(2)}) collective-permute-start(bf16[256,768]{1,0:T(8,128)(2,1)} %collective-permute-done.11.g2), channel_id=1, source_target_pairs={{0,1},{1,0},{2,3},{3,2},{4,5},{5,4},{6,7},{7,6},{8,9},{9,8},{10,11... | collective-permute-start | bytes 1179656 | tf_op jit(solution)/shard_map/ppermute | solution.py:26
  23.1 16.4 %copy-start.13 = (s32[1,1024,1]{1,2,0:T(1,128)S(1)}, s32[1,1024,1]{1,2,0:T(1,128)}, u32[]{:S(2)}) copy-start(s32[1,1024,1]{1,2,0:T(1,128)} %param.16) | copy-start | bytes 12292
  23.1 18.5 %copy-start.19 = (bf16[256,768]{1,0:T(8,128)(2,1)S(1)}, bf16[256,768]{1,0:T(8,128)(2,1)}, u32[]{:S(2)}) copy-start(bf16[256,768]{1,0:T(8,128)(2,1)} %g0.1) | copy-start | bytes 1179652
  38.9 28.8 %copy-start.20 = (bf16[1536,128]{1,0:T(8,128)(2,1)}, bf16[1536,128]{1,0:T(8,128)(2,1)S(1)}, u32[]{:S(2)}) copy-start(bf16[1536,128]{1,0:T(8,128)(2,1)S(1)} %get-tuple-element.54.c0.ctx) | copy-start | bytes 1179652
  38.9 21.9 %copy-start.38 = (f32[768]{0:T(1024)S(1)}, f32[768]{0:T(1024)}, u32[]{:S(2)}) copy-start(f32[768]{0:T(1024)} %param.21) | copy-start | bytes 9220
  38.9 14.8 %collective-permute-start.4 = (bf16[1536,128]{1,0:T(8,128)(2,1)S(1)}, bf16[1536,128]{1,0:T(8,128)(2,1)S(1)}, u32[]{:S(2)}, u32[]{:S(2)}) collective-permute-start(bf16[1536,128]{1,0:T(8,128)(2,1)S(1)} %get-tuple-element.54.c0.ctx), channel_id=1, source_target_pairs={{0,2},{2,0},{1,3},{3,1},{4,6},{6,4},{5,7},{7,5},{8,10},{10,8},{9,1... | collective-permute-start | bytes 1179656 | tf_op jit(solution)/shard_map/ppermute | solution.py:30
  45.6 23.0 %all-to-all-start.1 = ((bf16[8,40,768]{2,1,0:T(8,128)(2,1)}), bf16[8,40,768]{2,1,0:T(8,128)(2,1)S(1)}, u32[]{:S(2)}, u32[]{:S(2)}) async-start(bf16[8,40,768]{2,1,0:T(8,128)(2,1)} %bitcast.8), calls=%async_computation.1 | async-start | bytes 983040 | tf_op jit(solution)/shard_map/all_to_all | solution.py:473
  52.2 8.6 %collective-permute-start.7 = (bf16[192,768]{1,0:T(8,128)(2,1)S(1)}, bf16[192,768]{1,0:T(8,128)(2,1)S(1)}, u32[]{:S(2)}, u32[]{:S(2)}) collective-permute-start(bf16[192,768]{1,0:T(8,128)(2,1)S(1)} %copy-done.25), channel_id=1, source_target_pairs={{0,2},{2,0},{1,3},{3,1},{4,6},{6,4},{5,7},{7,5},{8,10},{10,8},{9,1... | collective-permute-start | bytes 884744 | tf_op jit(solution)/shard_map/ppermute | solution.py:30
  53.7 8.7 %collective-permute-start.3 = (bf16[1536,128]{1,0:T(8,128)(2,1)S(1)}, bf16[1536,128]{1,0:T(8,128)(2,1)S(1)}, u32[]{:S(2)}, u32[]{:S(2)}) collective-permute-start(bf16[1536,128]{1,0:T(8,128)(2,1)S(1)} %get-tuple-element.54.c0.ctx), channel_id=1, source_target_pairs={{0,1},{1,0},{2,3},{3,2},{4,5},{5,4},{6,7},{7,6},{8,9},{9,8},{10,11... | collective-permute-start | bytes 1179656 | tf_op jit(solution)/shard_map/ppermute | solution.py:26
  53.7 8.7 %collective-permute-start.5 = (bf16[1536,128]{1,0:T(8,128)(2,1)S(1)}, bf16[1536,128]{1,0:T(8,128)(2,1)S(1)}, u32[]{:S(2)}, u32[]{:S(2)}) collective-permute-start(bf16[1536,128]{1,0:T(8,128)(2,1)S(1)} %collective-permute-done.4.c2), channel_id=1, source_target_pairs={{0,1},{1,0},{2,3},{3,2},{4,5},{5,4},{6,7},{7,6},{8,9},{9,8},{10,11... | collective-permute-start | bytes 1179656 | tf_op jit(solution)/shard_map/ppermute | solution.py:26
  54.2 6.6 %collective-permute-start.6 = (bf16[192,768]{1,0:T(8,128)(2,1)S(1)}, bf16[192,768]{1,0:T(8,128)(2,1)S(1)}, u32[]{:S(2)}, u32[]{:S(2)}) collective-permute-start(bf16[192,768]{1,0:T(8,128)(2,1)S(1)} %copy-done.25), channel_id=1, source_target_pairs={{0,1},{1,0},{2,3},{3,2},{4,5},{5,4},{6,7},{7,6},{8,9},{9,8},{10,11... | collective-permute-start | bytes 884744 | tf_op jit(solution)/shard_map/ppermute | solution.py:26
  60.8 1.6 collective-permute-start.8
  63.8 34.1 %copy-start.37 = (bf16[768,16]{0,1:T(8,128)(2,1)S(1)}, bf16[768,16]{0,1:T(8,128)(2,1)}, u32[]{:S(2)}) copy-start(bf16[768,16]{0,1:T(8,128)(2,1)} %param.22) | copy-start | bytes 73732
  68.6 39.7 %copy-start.29 = (bf16[8,40,768]{2,1,0:T(8,128)(2,1)}, bf16[8,40,768]{2,1,0:T(8,128)(2,1)S(1)}, u32[]{:S(2)}) copy-start(bf16[8,40,768]{2,1,0:T(8,128)(2,1)S(1)} %all-to-all-done.1) | copy-start | bytes 1474564
  68.6 18.9 %all-to-all-start = ((bf16[8,40,768]{2,1,0:T(8,128)(2,1)}), bf16[8,40,768]{2,1,0:T(8,128)(2,1)S(1)}, u32[]{:S(2)}, u32[]{:S(2)}) async-start(bf16[8,40,768]{2,1,0:T(8,128)(2,1)} %bitcast.6), calls=%async_computation | async-start | bytes 983040 | tf_op jit(solution)/shard_map/all_to_all | solution.py:473
  74.6 14.4 %collective-permute-start.17 = (bf16[320,768]{1,0:T(8,128)(2,1)S(1)}, bf16[320,768]{1,0:T(8,128)(2,1)S(1)}, u32[]{:S(2)}, u32[]{:S(2)}) collective-permute-start(bf16[320,768]{1,0:T(8,128)(2,1)S(1)} %bitcast.45), channel_id=1, source_target_pairs={{0,2},{2,0},{1,3},{3,1},{4,6},{6,4},{5,7},{7,5},{8,10},{10,8},{9,1... | collective-permute-start | bytes 1474568 | tf_op jit(solution)/shard_map/ppermute | solution.py:30
  87.5 20.8 %copy-start.30 = (bf16[8,40,768]{2,1,0:T(8,128)(2,1)}, bf16[8,40,768]{2,1,0:T(8,128)(2,1)S(1)}, u32[]{:S(2)}) copy-start(bf16[8,40,768]{2,1,0:T(8,128)(2,1)S(1)} %all-to-all-done) | copy-start | bytes 1474564
  87.5 10.5 %collective-permute-start.15 = (bf16[320,768]{1,0:T(8,128)(2,1)S(1)}, bf16[320,768]{1,0:T(8,128)(2,1)S(1)}, u32[]{:S(2)}, u32[]{:S(2)}) collective-permute-start(bf16[320,768]{1,0:T(8,128)(2,1)S(1)} %bitcast.48), channel_id=1, source_target_pairs={{0,2},{2,0},{1,3},{3,1},{4,6},{6,4},{5,7},{7,5},{8,10},{10,8},{9,1... | collective-permute-start | bytes 1474568 | tf_op jit(solution)/shard_map/ppermute | solution.py:30
  89.0 10.9 %collective-permute-start.18 = (bf16[320,768]{1,0:T(8,128)(2,1)S(1)}, bf16[320,768]{1,0:T(8,128)(2,1)}, u32[]{:S(2)}, u32[]{:S(2)}) collective-permute-start(bf16[320,768]{1,0:T(8,128)(2,1)S(1)} %collective-permute-done.17.g0), channel_id=1, source_target_pairs={{0,1},{1,0},{2,3},{3,2},{4,5},{5,4},{6,7},{7,6},{8,9},{9,8},{10,11... | collective-permute-start | bytes 1474568 | tf_op jit(solution)/shard_map/ppermute | solution.py:26
  97.9 2.0 collective-permute-start.16
  99.3 10.1 %collective-permute-start.13 = (bf16[320,768]{1,0:T(8,128)(2,1)S(1)}, bf16[320,768]{1,0:T(8,128)(2,1)}, u32[]{:S(2)}, u32[]{:S(2)}) collective-permute-start(bf16[320,768]{1,0:T(8,128)(2,1)S(1)} %bitcast.46), channel_id=1, source_target_pairs={{0,1},{1,0},{2,3},{3,2},{4,5},{5,4},{6,7},{7,6},{8,9},{9,8},{10,11... | collective-permute-start | bytes 1474568 | tf_op jit(solution)/shard_map/ppermute | solution.py:26
  99.8 9.6 %collective-permute-start.9 = (bf16[320,768]{1,0:T(8,128)(2,1)S(1)}, bf16[320,768]{1,0:T(8,128)(2,1)}, u32[]{:S(2)}, u32[]{:S(2)}) collective-permute-start(bf16[320,768]{1,0:T(8,128)(2,1)S(1)} %bitcast.49), channel_id=1, source_target_pairs={{0,1},{1,0},{2,3},{3,2},{4,5},{5,4},{6,7},{7,6},{8,9},{9,8},{10,11... | collective-permute-start | bytes 1474568 | tf_op jit(solution)/shard_map/ppermute | solution.py:26
  108.3 9.8 %collective-permute-start.25 = (bf16[320,768]{1,0:T(8,128)(2,1)}, bf16[320,768]{1,0:T(8,128)(2,1)S(1)}, u32[]{:S(2)}, u32[]{:S(2)}) collective-permute-start(bf16[320,768]{1,0:T(8,128)(2,1)} %get-tuple-element.69), channel_id=1, source_target_pairs={{0,1},{1,0},{2,3},{3,2},{4,5},{5,4},{6,7},{7,6},{8,9},{9,8},{10,11... | collective-permute-start | bytes 1474568 | tf_op jit(solution)/shard_map/ppermute | solution.py:26
  117.9 37.4 %copy-start.32 = (bf16[320,768]{1,0:T(8,128)(2,1)S(1)}, bf16[320,768]{1,0:T(8,128)(2,1)}, u32[]{:S(2)}) copy-start(bf16[320,768]{1,0:T(8,128)(2,1)} %get-tuple-element.60) | copy-start | bytes 1474564
  117.9 2.1 collective-permute-start.24
  118.2 49.9 %copy-start.35 = (f32[16,768]{1,0:T(8,128)S(1)}, f32[16,768]{1,0:T(8,128)}, u32[]{:S(2)}) copy-start(f32[16,768]{1,0:T(8,128)} %get-tuple-element.74) | copy-start | bytes 147460
  118.2 49.9 %copy-start.36 = (f32[16,768]{1,0:T(8,128)S(1)}, f32[16,768]{1,0:T(8,128)}, u32[]{:S(2)}) copy-start(f32[16,768]{1,0:T(8,128)} %get-tuple-element.73) | copy-start | bytes 147460
  118.2 13.6 %collective-permute-start.26 = (bf16[320,768]{1,0:T(8,128)(2,1)S(1)}, bf16[320,768]{1,0:T(8,128)(2,1)S(1)}, u32[]{:S(2)}, u32[]{:S(2)}) collective-permute-start(bf16[320,768]{1,0:T(8,128)(2,1)S(1)} %add.53), channel_id=1, source_target_pairs={{0,2},{2,0},{1,3},{3,1},{4,6},{6,4},{5,7},{7,5},{8,10},{10,8},{9,1... | collective-permute-start | bytes 1474568 | tf_op jit(solution)/shard_map/ppermute | solution.py:30
  131.9 44.3 %copy-start.34 = (bf16[320,768]{1,0:T(8,128)(2,1)S(1)}, bf16[320,768]{1,0:T(8,128)(2,1)}, u32[]{:S(2)}) copy-start(bf16[320,768]{1,0:T(8,128)(2,1)} %get-tuple-element.58) | copy-start | bytes 1474564
  133.9 19.9 %all-to-all-start.3 = ((bf16[8,40,768]{2,1,0:T(8,128)(2,1)}), bf16[8,40,768]{2,1,0:T(8,128)(2,1)S(1)}, u32[]{:S(2)}, u32[]{:S(2)}) async-start(bf16[8,40,768]{2,1,0:T(8,128)(2,1)} %bitcast.14), calls=%async_computation.3 | async-start | bytes 983040 | tf_op jit(solution)/shard_map/all_to_all | solution.py:473
  141.4 13.9 %collective-permute-start.19 = (bf16[320,768]{1,0:T(8,128)(2,1)}, bf16[320,768]{1,0:T(8,128)(2,1)S(1)}, u32[]{:S(2)}, u32[]{:S(2)}) collective-permute-start(bf16[320,768]{1,0:T(8,128)(2,1)} %get-tuple-element.61), channel_id=1, source_target_pairs={{0,1},{1,0},{2,3},{3,2},{4,5},{5,4},{6,7},{7,6},{8,9},{9,8},{10,11... | collective-permute-start | bytes 1474568 | tf_op jit(solution)/shard_map/ppermute | solution.py:26
  153.8 23.2 %copy-start.31 = (bf16[8,40,768]{2,1,0:T(8,128)(2,1)}, bf16[8,40,768]{2,1,0:T(8,128)(2,1)S(1)}, u32[]{:S(2)}) copy-start(bf16[8,40,768]{2,1,0:T(8,128)(2,1)S(1)} %all-to-all-done.3) | copy-start | bytes 1474564
  153.8 14.3 %collective-permute-start.28 = (bf16[320,768]{1,0:T(8,128)(2,1)S(1)}, bf16[320,768]{1,0:T(8,128)(2,1)}, u32[]{:S(2)}, u32[]{:S(2)}) collective-permute-start(bf16[320,768]{1,0:T(8,128)(2,1)S(1)} %bitcast.51), channel_id=1, source_target_pairs={{0,2},{2,0},{1,3},{3,1},{4,6},{6,4},{5,7},{7,5},{8,10},{10,8},{9,1... | collective-permute-start | bytes 1474568 | tf_op jit(solution)/shard_map/ppermute | solution.py:30
  155.3 20.8 %collective-permute-start.14 = (bf16[320,768]{1,0:T(8,128)(2,1)}, bf16[320,768]{1,0:T(8,128)(2,1)S(1)}, u32[]{:S(2)}, u32[]{:S(2)}) collective-permute-start(bf16[320,768]{1,0:T(8,128)(2,1)} %get-tuple-element.59), channel_id=1, source_target_pairs={{0,1},{1,0},{2,3},{3,2},{4,5},{5,4},{6,7},{7,6},{8,9},{9,8},{10,11... | collective-permute-start | bytes 1474568 | tf_op jit(solution)/shard_map/ppermute | solution.py:26
  155.4 20.7 %collective-permute-start.20 = (bf16[320,768]{1,0:T(8,128)(2,1)S(1)}, bf16[320,768]{1,0:T(8,128)(2,1)S(1)}, u32[]{:S(2)}, u32[]{:S(2)}) collective-permute-start(bf16[320,768]{1,0:T(8,128)(2,1)S(1)} %add.50), channel_id=1, source_target_pairs={{0,2},{2,0},{1,3},{3,1},{4,6},{6,4},{5,7},{7,5},{8,10},{10,8},{9,1... | collective-permute-start | bytes 1474568 | tf_op jit(solution)/shard_map/ppermute | solution.py:30
  156.1 28.7 %collective-permute-start.27 = (bf16[320,768]{1,0:T(8,128)(2,1)S(1)}, bf16[320,768]{1,0:T(8,128)(2,1)}, u32[]{:S(2)}, u32[]{:S(2)}) collective-permute-start(bf16[320,768]{1,0:T(8,128)(2,1)S(1)} %bitcast.52), channel_id=1, source_target_pairs={{0,1},{1,0},{2,3},{3,2},{4,5},{5,4},{6,7},{7,6},{8,9},{9,8},{10,11... | collective-permute-start | bytes 1474568 | tf_op jit(solution)/shard_map/ppermute | solution.py:26
  168.1 16.7 %collective-permute-start.29 = (bf16[320,768]{1,0:T(8,128)(2,1)}, bf16[320,768]{1,0:T(8,128)(2,1)}, u32[]{:S(2)}, u32[]{:S(2)}) collective-permute-start(bf16[320,768]{1,0:T(8,128)(2,1)} %collective-permute-done.28.b2), channel_id=1, source_target_pairs={{0,1},{1,0},{2,3},{3,2},{4,5},{5,4},{6,7},{7,6},{8,9},{9,8},{10,11... | collective-permute-start | bytes 1474568 | tf_op jit(solution)/shard_map/ppermute | solution.py:26
  168.1 1.9 collective-permute-start.30
  170.0 5.5 %collective-permute-start.31 = (f32[16,768]{1,0:T(8,128)S(1)}, f32[16,768]{1,0:T(8,128)S(1)}, u32[]{:S(2)}, u32[]{:S(2)}) collective-permute-start(f32[16,768]{1,0:T(8,128)S(1)} %add.56), channel_id=1, source_target_pairs={{0,2},{2,0},{1,3},{3,1},{4,6},{6,4},{5,7},{7,5},{8,10},{10,8},{9,1... | collective-permute-start | bytes 147464 | tf_op jit(solution)/shard_map/ppermute | solution.py:30
  177.0 48.9 %all-to-all-start.2 = ((bf16[8,40,768]{2,1,0:T(8,128)(2,1)}), bf16[8,40,768]{2,1,0:T(8,128)(2,1)S(1)}, u32[]{:S(2)}, u32[]{:S(2)}) async-start(bf16[8,40,768]{2,1,0:T(8,128)(2,1)} %bitcast.12), calls=%async_computation.2 | async-start | bytes 983040 | tf_op jit(solution)/shard_map/all_to_all | solution.py:473
  226.0 25.6 %copy-start = (bf16[1024,768]{1,0:T(8,128)(2,1)S(1)}, bf16[1024,768]{1,0:T(8,128)(2,1)}, u32[]{:S(2)}) copy-start(bf16[1024,768]{1,0:T(8,128)(2,1)} %get-tuple-element.72.normed) | copy-start | bytes 4718596
  246.0 14.5 %copy-start.39 = (f32[32,128]{1,0:T(8,128)S(1)}, f32[32,128]{1,0:T(8,128)}, u32[]{:S(2)}) copy-start(f32[32,128]{1,0:T(8,128)} %get-tuple-element.84) | copy-start | bytes 49156
  246.0 20.6 %all-to-all-start.6 = ((bf16[8,56,768]{2,1,0:T(8,128)(2,1)}), bf16[8,56,768]{2,1,0:T(8,128)(2,1)}, u32[]{:S(2)}, u32[]{:S(2)}) async-start(bf16[8,56,768]{2,1,0:T(8,128)(2,1)} %bitcast.43), calls=%async_computation.6 | async-start | bytes 1376256 | tf_op jit(solution)/shard_map/all_to_all | solution.py:473
  257.9 15.4 %copy-start.18 = (bf16[512,768]{1,0:T(8,128)(2,1)S(1)}, bf16[512,768]{1,0:T(8,128)(2,1)}, u32[]{:S(2)}) copy-start(bf16[512,768]{1,0:T(8,128)(2,1)} %copy-done.17) | copy-start | bytes 2359300
  257.9 1.2 collective-permute-start.34
  259.1 3.6 %collective-permute-start.35 = (f32[1,768]{1,0:T(1,128)S(1)}, f32[1,768]{1,0:T(1,128)S(1)}, u32[]{:S(2)}, u32[]{:S(2)}) collective-permute-start(f32[1,768]{1,0:T(1,128)S(1)} %add.59), channel_id=1, source_target_pairs={{0,2},{2,0},{1,3},{3,1},{4,6},{6,4},{5,7},{7,5},{8,10},{10,8},{9,1... | collective-permute-start | bytes 9224 | tf_op jit(solution)/shard_map/ppermute | solution.py:30
  267.6 30.5 %copy-start.3 = (bf16[512,768]{1,0:T(8,128)(2,1)S(1)}, bf16[512,768]{1,0:T(8,128)(2,1)}, u32[]{:S(2)}) copy-start(bf16[512,768]{1,0:T(8,128)(2,1)} %copy-done.2) | copy-start | bytes 2359300
  267.6 23.0 %all-to-all-start.5 = ((bf16[8,64,768]{2,1,0:T(8,128)(2,1)}), bf16[8,64,768]{2,1,0:T(8,128)(2,1)}, u32[]{:S(2)}, u32[]{:S(2)}) async-start(bf16[8,64,768]{2,1,0:T(8,128)(2,1)} %broadcast_in_dim.29), calls=%async_computation.5 | async-start | bytes 1572864 | tf_op jit(solution)/shard_map/all_to_all | solution.py:473
  273.3 24.8 %collective-permute-start.32 = (bf16[512,768]{1,0:T(8,128)(2,1)S(1)}, bf16[512,768]{1,0:T(8,128)(2,1)}, u32[]{:S(2)}, u32[]{:S(2)}) collective-permute-start(bf16[512,768]{1,0:T(8,128)(2,1)S(1)} %copy-done.18), channel_id=1, source_target_pairs={{0,1},{1,0},{2,3},{3,2},{4,5},{5,4},{6,7},{7,6},{8,9},{9,8},{10,11... | collective-permute-start | bytes 2359304 | tf_op jit(solution)/shard_map/ppermute | solution.py:26
  273.3 24.3 %collective-permute-start.22 = (bf16[320,768]{1,0:T(8,128)(2,1)S(1)}, bf16[320,768]{1,0:T(8,128)(2,1)S(1)}, u32[]{:S(2)}, u32[]{:S(2)}) collective-permute-start(bf16[320,768]{1,0:T(8,128)(2,1)S(1)} %bitcast.35), channel_id=1, source_target_pairs={{0,2},{2,0},{1,3},{3,1},{4,6},{6,4},{5,7},{7,5},{8,10},{10,8},{9,1... | collective-permute-start | bytes 1474568 | tf_op jit(solution)/shard_map/ppermute | solution.py:30
  291.4 23.9 %all-to-all-start.7 = ((bf16[8,56,768]{2,1,0:T(8,128)(2,1)}), bf16[8,56,768]{2,1,0:T(8,128)(2,1)}, u32[]{:S(2)}, u32[]{:S(2)}) async-start(bf16[8,56,768]{2,1,0:T(8,128)(2,1)} %broadcast_in_dim.30), calls=%async_computation.7 | async-start | bytes 1376256 | tf_op jit(solution)/shard_map/all_to_all | solution.py:473
  297.5 13.0 %collective-permute-start.21 = (bf16[320,768]{1,0:T(8,128)(2,1)S(1)}, bf16[320,768]{1,0:T(8,128)(2,1)S(1)}, u32[]{:S(2)}, u32[]{:S(2)}) collective-permute-start(bf16[320,768]{1,0:T(8,128)(2,1)S(1)} %bitcast.36), channel_id=1, source_target_pairs={{0,1},{1,0},{2,3},{3,2},{4,5},{5,4},{6,7},{7,6},{8,9},{9,8},{10,11... | collective-permute-start | bytes 1474568 | tf_op jit(solution)/shard_map/ppermute | solution.py:26
  297.6 12.9 %collective-permute-start.23 = (bf16[320,768]{1,0:T(8,128)(2,1)S(1)}, bf16[320,768]{1,0:T(8,128)(2,1)S(1)}, u32[]{:S(2)}, u32[]{:S(2)}) collective-permute-start(bf16[320,768]{1,0:T(8,128)(2,1)S(1)} %collective-permute-done.22.f2), channel_id=1, source_target_pairs={{0,1},{1,0},{2,3},{3,2},{4,5},{5,4},{6,7},{7,6},{8,9},{9,8},{10,11... | collective-permute-start | bytes 1474568 | tf_op jit(solution)/shard_map/ppermute | solution.py:26
  299.4 13.0 %collective-permute-start.33 = (bf16[256,768]{1,0:T(8,128)(2,1)S(1)}, bf16[256,768]{1,0:T(8,128)(2,1)S(1)}, u32[]{:S(2)}, u32[]{:S(2)}) collective-permute-start(bf16[256,768]{1,0:T(8,128)(2,1)S(1)} %get-tuple-element.118), channel_id=1, source_target_pairs={{0,2},{2,0},{1,3},{3,1},{4,6},{6,4},{5,7},{7,5},{8,10},{10,8},{9,1... | collective-permute-start | bytes 1179656 | tf_op jit(solution)/shard_map/ppermute | solution.py:30
  (23 other events, 85.9 us)
